TPU v7x, 32 devices: a whole 2x2x4 slice. The times are simulated.
32 devices in a mesh: prompt: 8 (over z, x), seq: 4 (over y, core).
Axes of the slice: x: 2, y: 2, z: 4, core: 2. Of those that a mesh axis runs over, the one named last changes fastest.
Arguments:
- queries: bfloat16 [8, 2048, 1024], P('prompt', 'seq'), may hold values from -5 to 5
- resp_kv: bfloat16 [8, 2048, 256], P('prompt', 'seq'), may hold values from -16 to 16
- prefix_kv: bfloat16 [8, 192, 256], P('prompt', 'seq'), may hold values from -16 to 16
- lengths: int32 [8, 4], P('prompt'), may hold values from 256 to 512, as said below
- upstream: bfloat16 [8, 2048, 1024], P('prompt', 'seq'), may hold values from -6 to 6
Outputs:
- attended: bfloat16 [8, 2048, 1024], P('prompt', 'seq')
- grad_queries: bfloat16 [8, 2048, 1024], P('prompt', 'seq')
- grad_resp_kv: float32 [8, 2048, 256], P('prompt', 'seq')
- grad_prefix_kv: float32 [8, 192, 256], P('prompt', 'seq')
Inputs may be any that keep to these rules, and one draw needn't show every extreme that they name: `lengths`: each prompt's 4 responses fill its slots in order from slot 0; one response of every prompt has exactly 512 tokens.
All inputs are finite; a program needn't handle non-finite values.
Results may differ from a plain program's by a relative error of at most 0.011.
Values may be sent and summed in bfloat16 or wider, within the bound.
A program may use at most 192 MiB of HBM per device.

v0:
```python
import math

import jax
import jax.numpy as jnp
from jax import lax
from jax.sharding import PartitionSpec as P


def shifted(block, axis, distance):
    devices = range(lax.axis_size(axis))
    route = [(i - distance, i) for i in devices if i - distance in devices]
    return lax.ppermute(block, axis, route)


def slot_segments(resp_ends, slot_ids):
    counted = jnp.sum((slot_ids[:, None] >= resp_ends[None, :]).astype(jnp.int32), axis=1)
    return jnp.where(slot_ids < 0, -1, counted)


def block_terms(query_block, grad_block, key_part, value_part, visible, live_rows, score_scale):
    scores = (
        jnp.einsum("rgd,kd->rgk", query_block, key_part, preferred_element_type=jnp.float32)
        * score_scale
    )
    scores = jnp.where(visible[:, None, :], scores, -jnp.inf)
    row_max = jnp.max(scores, axis=-1, keepdims=True)
    weights = jnp.exp(scores - row_max)
    row_total = jnp.sum(weights, axis=-1, keepdims=True)
    mixed = (
        jnp.einsum(
            "rgk,kd->rgd",
            weights.astype(jnp.bfloat16),
            value_part,
            preferred_element_type=jnp.float32,
        )
        / row_total
    )
    attended = (mixed * live_rows[:, None, None]).astype(jnp.bfloat16)
    log_total = row_max + jnp.log(row_total)
    probs = jnp.exp(scores - log_total)
    delta = jnp.sum(
        grad_block.astype(jnp.float32) * attended.astype(jnp.float32), axis=-1, keepdims=True
    )
    dprobs = jnp.einsum("rgd,kd->rgk", grad_block, value_part, preferred_element_type=jnp.float32)
    dscores = (probs * (dprobs - delta)).astype(jnp.bfloat16)
    grad_query = (
        jnp.einsum("rgk,kd->rgd", dscores, key_part, preferred_element_type=jnp.float32)
        * score_scale
    ).astype(jnp.bfloat16)
    return (attended, grad_query, dscores, probs.astype(jnp.bfloat16))


def body(queries, resp_kv, prefix_kv, lengths, upstream):
    shard_rows = queries.shape[1]
    head_dim = resp_kv.shape[2] // 2
    head_count = queries.shape[2] // head_dim
    responses = lengths.shape[1]
    score_scale = head_dim ** (-0.5)
    shard_index = lax.axis_index("seq")
    resp_ends = jnp.cumsum(lengths[0])
    positions = shard_index * shard_rows + jnp.arange(shard_rows, dtype=jnp.int32)
    own_seg = slot_segments(resp_ends, positions)
    prev_seg = slot_segments(resp_ends, positions - shard_rows)
    live_rows = (own_seg < responses).astype(jnp.float32)
    live_total = lax.psum(jnp.sum(lengths[0]).astype(jnp.float32), "prompt")
    factor = jnp.float32(lax.axis_size("prompt") * lax.axis_size("seq") * shard_rows) / live_total
    prefix_all = lax.all_gather(prefix_kv[0], "seq", axis=0, tiled=True)
    previous = shifted(resp_kv[0], "seq", 1)
    prefix_len = prefix_all.shape[0]
    key_vals = jnp.concatenate([prefix_all, previous, resp_kv[0]], axis=0)
    key_slots = jnp.concatenate([positions - shard_rows, positions])
    key_segs = jnp.concatenate([prev_seg, own_seg])
    same_resp = (key_segs[None, :] == own_seg[:, None]) & (key_slots[None, :] <= positions[:, None])
    visible = jnp.concatenate([jnp.ones((shard_rows, prefix_len), jnp.bool_), same_resp], axis=1)
    key_part = key_vals[:, :head_dim]
    value_part = key_vals[:, head_dim:]
    query_three = queries[0].reshape(shard_rows, head_count, head_dim)
    scaled_live = factor * live_rows
    grad_out = (
        upstream[0].reshape(shard_rows, head_count, head_dim).astype(jnp.float32)
        * scaled_live[:, None, None]
    ).astype(jnp.bfloat16)
    head_group = math.gcd(head_count, max(1, 512 // shard_rows))
    out_parts = []
    query_grads = []
    key_grads = jnp.zeros((prefix_len + 2 * shard_rows, head_dim), jnp.float32)
    value_grads = jnp.zeros((prefix_len + 2 * shard_rows, head_dim), jnp.float32)
    for first_head in range(0, head_count, head_group):
        query_block = query_three[:, first_head : first_head + head_group]
        grad_block = grad_out[:, first_head : first_head + head_group]
        attended, grad_query, dscores, probs_low = block_terms(
            query_block, grad_block, key_part, value_part, visible, live_rows, score_scale
        )
        key_grads = key_grads + jnp.einsum(
            "rgk,rgd->kd", dscores, query_block, preferred_element_type=jnp.float32
        )
        value_grads = value_grads + jnp.einsum(
            "rgk,rgd->kd", probs_low, grad_block, preferred_element_type=jnp.float32
        )
        out_parts.append(attended)
        query_grads.append(grad_query)
    kv_grads = jnp.concatenate([key_grads * score_scale, value_grads], axis=1)
    prefix_grads = lax.psum_scatter(kv_grads[:prefix_len], "seq", scatter_dimension=0, tiled=True)
    prev_grads = kv_grads[prefix_len : prefix_len + shard_rows]
    own_grads = kv_grads[prefix_len + shard_rows :]
    returned = shifted(prev_grads.astype(jnp.bfloat16), "seq", -1).astype(prev_grads.dtype)
    grad_resp = own_grads + returned
    attended_all = jnp.concatenate(out_parts, axis=1).reshape(shard_rows, head_count * head_dim)
    query_grad_all = jnp.concatenate(query_grads, axis=1).reshape(shard_rows, head_count * head_dim)
    return (attended_all[None], query_grad_all[None], grad_resp[None], prefix_grads[None])


def solution(mesh):
    in_specs = (
        P("prompt", "seq", None),
        P("prompt", "seq", None),
        P("prompt", "seq", None),
        P("prompt", None),
        P("prompt", "seq", None),
    )
    out_specs = (
        P("prompt", "seq", None),
        P("prompt", "seq", None),
        P("prompt", "seq", None),
        P("prompt", "seq", None),
    )
    return jax.shard_map(body, mesh=mesh, in_specs=in_specs, out_specs=out_specs, check_vma=False)
```

profile of v0, /device:TPU:1, one launch (start us, length us, event | category | flops | bytes accessed | tf_op | source)
XLA Modules:
  0.0 108.6 jit_solution(6740361414578981116)
XLA Ops:
  7.2 4.7 %collective-permute-start = (bf16[512,256]{1,0:T(8,128)(2,1)}, bf16[512,256]{1,0:T(8,128)(2,1)S(1)}, u32[]{:S(2)}, u32[]{:S(2)}) collective-permute-start(bf16[512,256]{1,0:T(8,128)(2,1)} %bitcast.231), channel_id=1, source_target_pairs={{0,1},{1,2},{2,3},{4,5},{5,6},{6,7},{8,9},{9,10},{10,11},{12,13},{... | collective-permute-start | bytes 786440 | tf_op jit(solution)/shard_map/ppermute | solution.py:12
  11.9 1.3 %reduce_sum.181 = s32[]{:T(128)} reduce(s32[1,4]{1,0:T(1,128)} %param.8, s32[]{:T(128)} %constant.14.clone.1), dimensions={0,1}, to_apply=%region_19.20 | reduce | flops 3 | bytes 24 | tf_op jit(solution)/shard_map/reduce_sum | solution.py:65
  13.9 18.4 %psum.7 = f32[]{:T(128)} all-reduce(f32[]{:T(128)S(6)} %convert_element_type.306), channel_id=1, replica_groups=mesh['prompt'=8,'seq'=4] {'prompt'}, use_global_device_ids=true, to_apply=%region_20.21 | all-reduce | flops 1 | bytes 8 | tf_op jit(solution)/shard_map/psum | solution.py:65
  32.3 0.8 reduce-window.8
  33.9 1.5 %copy.27 = bf16[1,512,1024]{1,2,0:T(8,128)(2,1)S(1)} copy(bf16[1,512,1024]{2,1,0:T(8,128)(2,1)} %param.5) | data formatting | bytes 2097152 | tf_op args[0]
  35.4 1.7 %copy.36 = f32[1,512,1024]{1,2,0:T(8,128)} copy(bf16[1,512,1024]{2,1,0:T(8,128)(2,1)S(1)} %copy-done.13) | data formatting | bytes 3145728 | tf_op jit(solution)/shard_map/convert_element_type | solution.py:80
  37.1 1.9 %multiply_convert_fusion = bf16[512,8,128]{0,2,1:T(8,128)(2,1)S(1)} fusion(f32[512,8,128]{0,2,1:T(8,128)} %bitcast.227, f32[512]{0:T(512)S(1)} %get-tuple-element.30), kind=kLoop, calls=%fused_computation.103 | loop fusion | flops 1048576 | bytes 3147776 | tf_op jit(solution)/shard_map/convert_element_type | solution.py:82
  39.0 7.6 %all-gather = bf16[1,192,256]{2,1,0:T(8,128)(2,1)S(1)} all-gather(bf16[1,48,256]{2,1,0:T(8,128)(2,1)S(1)} %copy-done.16), channel_id=2, replica_groups=mesh['prompt'=8,'seq'=4] {'seq'}, dimensions={1}, use_global_device_ids=true | all-gather | bytes 122880 | tf_op jit(solution)/shard_map/all_gather | solution.py:67
  46.7 0.8 compare_and_fusion
  60.6 0.6 fusion.24
  61.2 0.7 fusion.239
  61.8 1.0 fusion.217
  66.0 0.6 fusion.30
  66.6 0.6 fusion.29
  67.8 0.6 fusion.27
  68.4 0.6 fusion.26
  69.0 0.6 fusion.25
  70.1 0.6 fusion.31
  74.2 0.7 pad_maximum_fusion.1
  74.9 2.4 %copy.37 = bf16[1,512,1024]{2,1,0:T(8,128)(2,1)} copy(bf16[1,512,1024]{1,2,0:T(8,128)(2,1)} %bitcast.229) | data formatting | bytes 2097152
  77.3 2.5 %fusion.215 = bf16[512,8,128]{0,2,1:T(8,128)(2,1)} fusion(bf16[512,8,128]{0,2,1:T(8,128)(2,1)} %fusion.217, bf16[512,1216]{0,1:T(8,128)(2,1)} %copy-done.12, bf16[1216,256]{1,0:T(8,128)(2,1)S(1)} %pad_maximum_fusion), kind=kOutput, calls=%fused_computation.195 | convolution fusion | flops 159514624 | bytes 1687552 | tf_op jit(solution)/shard_map/rgk,kd->rgd/dot_general | solution.py:47
  79.8 1.0 fusion.213
  80.8 1.0 fusion.211
  81.9 1.0 fusion.209
  82.9 1.0 fusion.207
  84.0 1.0 fusion.205
  85.0 2.1 %collective-permute-start.1 = (bf16[512,256]{1,0:T(8,128)(2,1)S(1)}, bf16[512,256]{1,0:T(8,128)(2,1)}, u32[]{:S(2)}, u32[]{:S(2)}) collective-permute-start(bf16[512,256]{1,0:T(8,128)(2,1)S(1)} %fusion.219), channel_id=1, source_target_pairs={{1,0},{2,1},{3,2},{5,4},{6,5},{7,6},{9,8},{10,9},{11,10},{13,12},{... | collective-permute-start | bytes 786440 | tf_op jit(solution)/shard_map/ppermute | solution.py:12
  87.1 1.0 fusion.203
  88.2 2.3 %copy.38 = bf16[1,512,1024]{2,1,0:T(8,128)(2,1)} copy(bf16[1,512,1024]{1,2,0:T(8,128)(2,1)} %bitcast.228) | data formatting | bytes 2097152
  90.4 2.4 %collective-permute-done.1 = bf16[512,256]{1,0:T(8,128)(2,1)} collective-permute-done((bf16[512,256]{1,0:T(8,128)(2,1)S(1)}, bf16[512,256]{1,0:T(8,128)(2,1)}, u32[]{:S(2)}, u32[]{:S(2)}) %collective-permute-start.1) | collective-permute-done | bytes 262176 | tf_op jit(solution)/shard_map/ppermute | solution.py:12
  92.8 1.8 %fusion.222 = f32[1,512,256]{2,1,0:T(8,128)} fusion(f32[1216,128]{1,0:T(8,128)S(1)} %fusion.32, f32[1216,128]{1,0:T(8,128)S(1)} %convolution_add_fusion, bf16[512,256]{1,0:T(8,128)(2,1)} %collective-permute-done.1), kind=kLoop, calls=%fused_computation.203 | loop fusion | flops 393216 | bytes 2031616 | tf_op jit(solution)/shard_map/broadcast_in_dim | solution.py:110
  94.6 7.1 %reduce-scatter.2.cloned.1.call-done = f32[48,256]{1,0:T(8,128)} async-done(((f32[192,256]{1,0:T(8,128)}), f32[48,256]{1,0:T(8,128)}) %reduce-scatter.2.cloned.1.call-update) | async-done | bytes 49168 | tf_op jit(solution)/shard_map/reduce_scatter | solution.py:103
  (95 shorter events, 20.8 us)
Async XLA Ops:
  7.2 28.3 %copy-start.13 = (bf16[1,512,1024]{2,1,0:T(8,128)(2,1)S(1)}, bf16[1,512,1024]{2,1,0:T(8,128)(2,1)}, u32[]{:S(2)}) copy-start(bf16[1,512,1024]{2,1,0:T(8,128)(2,1)} %param.9) | copy-start | bytes 3145732
  7.2 94.6 %reduce-scatter.2.cloned.1.call-start = ((), (), s32[]{:S(2)}) async-start(), calls=%async_computation.1 | async-start | bytes 245760 | tf_op jit(solution)/shard_map/reduce_scatter | solution.py:103
  7.2 40.3 %collective-permute-start = (bf16[512,256]{1,0:T(8,128)(2,1)}, bf16[512,256]{1,0:T(8,128)(2,1)S(1)}, u32[]{:S(2)}, u32[]{:S(2)}) collective-permute-start(bf16[512,256]{1,0:T(8,128)(2,1)} %bitcast.231), channel_id=1, source_target_pairs={{0,1},{1,2},{2,3},{4,5},{5,6},{6,7},{8,9},{9,10},{10,11},{12,13},{... | collective-permute-start | bytes 786440 | tf_op jit(solution)/shard_map/ppermute | solution.py:12
  35.4 3.6 %copy-start.16 = (bf16[1,48,256]{2,1,0:T(8,128)(2,1)S(1)}, bf16[1,48,256]{2,1,0:T(8,128)(2,1)}, u32[]{:S(2)}) copy-start(bf16[1,48,256]{2,1,0:T(8,128)(2,1)} %param.7) | copy-start | bytes 73732
  37.1 10.4 %copy-start.15 = (bf16[1,512,256]{2,1,0:T(8,128)(2,1)S(1)}, bf16[1,512,256]{2,1,0:T(8,128)(2,1)}, u32[]{:S(2)}) copy-start(bf16[1,512,256]{2,1,0:T(8,128)(2,1)} %param.6) | copy-start | bytes 786436
  59.6 1.0 copy-start.14
  66.6 6.6 %copy-start = (bf16[512,1216]{0,1:T(8,128)(2,1)}, bf16[512,1216]{0,1:T(8,128)(2,1)S(1)}, u32[]{:S(2)}) copy-start(bf16[512,1216]{0,1:T(8,128)(2,1)S(1)} %fusion.30) | copy-start | bytes 3735556
  67.2 5.5 %copy-start.2 = (bf16[512,1216]{0,1:T(8,128)(2,1)}, bf16[512,1216]{0,1:T(8,128)(2,1)S(1)}, u32[]{:S(2)}) copy-start(bf16[512,1216]{0,1:T(8,128)(2,1)S(1)} %fusion.29) | copy-start | bytes 3735556
  67.8 4.4 %copy-start.6 = (bf16[512,1216]{0,1:T(8,128)(2,1)}, bf16[512,1216]{0,1:T(8,128)(2,1)S(1)}, u32[]{:S(2)}) copy-start(bf16[512,1216]{0,1:T(8,128)(2,1)S(1)} %fusion.28) | copy-start | bytes 3735556
  68.4 3.3 %copy-start.8 = (bf16[512,1216]{0,1:T(8,128)(2,1)}, bf16[512,1216]{0,1:T(8,128)(2,1)S(1)}, u32[]{:S(2)}) copy-start(bf16[512,1216]{0,1:T(8,128)(2,1)S(1)} %fusion.27) | copy-start | bytes 3735556
  69.0 2.2 %copy-start.10 = (bf16[512,1216]{0,1:T(8,128)(2,1)}, bf16[512,1216]{0,1:T(8,128)(2,1)S(1)}, u32[]{:S(2)}) copy-start(bf16[512,1216]{0,1:T(8,128)(2,1)S(1)} %fusion.26) | copy-start | bytes 3735556
  69.6 2.6 %copy-start.12 = (bf16[512,1216]{0,1:T(8,128)(2,1)}, bf16[512,1216]{0,1:T(8,128)(2,1)S(1)}, u32[]{:S(2)}) copy-start(bf16[512,1216]{0,1:T(8,128)(2,1)S(1)} %fusion.25) | copy-start | bytes 3735556
  70.7 3.0 %copy-start.4 = (bf16[512,1216]{0,1:T(8,128)(2,1)}, bf16[512,1216]{0,1:T(8,128)(2,1)S(1)}, u32[]{:S(2)}) copy-start(bf16[512,1216]{0,1:T(8,128)(2,1)S(1)} %fusion.31) | copy-start | bytes 3735556
  74.9 4.9 %copy-start.11 = (bf16[512,1216]{0,1:T(8,128)(2,1)S(1)}, bf16[512,1216]{0,1:T(8,128)(2,1)}, u32[]{:S(2)}) copy-start(bf16[512,1216]{0,1:T(8,128)(2,1)} %copy-done.10) | copy-start | bytes 3735556
  77.3 3.5 %copy-start.9 = (bf16[512,1216]{0,1:T(8,128)(2,1)S(1)}, bf16[512,1216]{0,1:T(8,128)(2,1)}, u32[]{:S(2)}) copy-start(bf16[512,1216]{0,1:T(8,128)(2,1)} %copy-done.8) | copy-start | bytes 3735556
  77.3 4.6 %copy-start.7 = (bf16[512,1216]{0,1:T(8,128)(2,1)S(1)}, bf16[512,1216]{0,1:T(8,128)(2,1)}, u32[]{:S(2)}) copy-start(bf16[512,1216]{0,1:T(8,128)(2,1)} %copy-done.6) | copy-start | bytes 3735556
  79.8 3.1 %copy-start.3 = (bf16[512,1216]{0,1:T(8,128)(2,1)S(1)}, bf16[512,1216]{0,1:T(8,128)(2,1)}, u32[]{:S(2)}) copy-start(bf16[512,1216]{0,1:T(8,128)(2,1)} %copy-done.2) | copy-start | bytes 3735556
  80.8 3.1 %copy-start.1 = (bf16[512,1216]{0,1:T(8,128)(2,1)S(1)}, bf16[512,1216]{0,1:T(8,128)(2,1)}, u32[]{:S(2)}) copy-start(bf16[512,1216]{0,1:T(8,128)(2,1)} %copy-done) | copy-start | bytes 3735556
  82.9 4.2 %copy-start.5 = (bf16[512,1216]{0,1:T(8,128)(2,1)S(1)}, bf16[512,1216]{0,1:T(8,128)(2,1)}, u32[]{:S(2)}) copy-start(bf16[512,1216]{0,1:T(8,128)(2,1)} %copy-done.4) | copy-start | bytes 3735556
  85.0 7.8 %collective-permute-start.1 = (bf16[512,256]{1,0:T(8,128)(2,1)S(1)}, bf16[512,256]{1,0:T(8,128)(2,1)}, u32[]{:S(2)}, u32[]{:S(2)}) collective-permute-start(bf16[512,256]{1,0:T(8,128)(2,1)S(1)} %fusion.219), channel_id=1, source_target_pairs={{1,0},{2,1},{3,2},{5,4},{6,5},{7,6},{9,8},{10,9},{11,10},{13,12},{... | collective-permute-start | bytes 786440 | tf_op jit(solution)/shard_map/ppermute | solution.py:12
Sparse Core Ops, SparseCore 0:
  85.1 16.5 reduce-scatter.1
where the time goes:
time: 110 us; the launch traced here: 109 us
  matrix products  31.1 us (28%)
  blocking collectives  26 us (24%)
  between operations  15.9 us (14%)
  other arithmetic  11.2 us (10%)
  waiting for transfers between devices  9.57 us (9%)
  local copies, waits for them, and re-layouts  7.99 us (7%)
  starting transfers between devices  6.79 us (6%)
    psum x1, blocking collectives, body(): live_total = lax.psum(jnp.sum(lengths[0]).astype(jnp.float32), 'prompt')  18.4 us
    dot_general x8, matrix products, block_terms(): jnp.einsum('rgk,kd->rgd', dscores, key_part, preferred_element_type=jnp.f...  9.74 us
    all_gather x1, blocking collectives, body(): prefix_all = lax.all_gather(prefix_kv[0], 'seq', axis=0, tiled=True)  7.65 us
    reduce_scatter x1, waiting for transfers between devices, body(): lax.psum_scatter(kv_grads[:prefix_len], 'seq', scatter_dimension=0, tiled...  7.15 us
    ppermute x2, starting transfers between devices, shifted(): return lax.ppermute(block, axis, route)  6.75 us
    unnamed x37, local copies, waits for them, and re-layouts  6.33 us
    dot_general x8, matrix products, block_terms(): jnp.einsum('rgd,kd->rgk', grad_block, value_part, preferred_element_type=...  4.62 us
    dot_general x8, matrix products, block_terms(): jnp.einsum('rgd,kd->rgk', query_block, key_part, preferred_element_type=j...  4.32 us
  transfers between devices with their start and end apart: 3, of which 2 were waited for; matrix products, arithmetic and copies ran while one was open for 12% of the time, Pallas kernels for 0%

commit v1 on v0

v1 whole, which is shorter than its diff:
```python
import functools
import math

import jax
import jax.numpy as jnp
from jax import lax
from jax.experimental import pallas as pl
from jax.experimental.pallas import tpu as pltpu
from jax.sharding import PartitionSpec as P

F32 = jnp.float32
BF16 = jnp.bfloat16
TILE = 128
HIDDEN = -1e30
PAIR = 2
ONES = 16


def mm(a, b):
    return lax.dot_general(a, b, (((1,), (0,)), ((), ())), preferred_element_type=F32)


def mm_nt(a, b):
    return lax.dot_general(a, b, (((1,), (1,)), ((), ())), preferred_element_type=F32)


def kernel(
    n_prompt,
    n_seq,
    lens_ref,
    q_hbm,
    kv_hbm,
    pkv_hbm,
    up_hbm,
    att_hbm,
    gq_hbm,
    gkv_hbm,
    gpf_hbm,
    q_ref,
    up_ref,
    win,
    pfx,
    win_kt,
    win_vt,
    pfx_kt,
    pfx_vt,
    bias,
    att,
    gq,
    acc,
    acc_p,
    ret_out,
    ret_in,
    gp_out,
    gp_in,
    gkv,
    gpf,
    lens_all,
    in_sem,
    out_sem,
    pf_send,
    pf_recv,
    prev_send,
    prev_recv,
    len_send,
    len_recv,
    ret_send,
    ret_recv,
    gp_send,
    gp_recv,
):
    rows = q_ref.shape[0]
    dim = win.shape[1] // 2
    heads = q_ref.shape[1] // dim
    tiles = rows // TILE
    block = pkv_hbm.shape[1]
    span = rows + TILE
    responses = lens_ref.shape[1]
    scale = dim ** (-0.5)
    my_p = lax.axis_index("prompt")
    me = lax.axis_index("seq")
    has_next = me < n_seq - 1
    has_prev = me > 0

    seq_peers = [lax.rem(me + d, n_seq) for d in range(1, n_seq)]
    prompt_peers = [lax.rem(my_p + d, n_prompt) for d in range(1, n_prompt)]

    barrier = pltpu.get_barrier_semaphore()
    for peer in seq_peers:
        pl.semaphore_signal(
            barrier, inc=1, device_id=(my_p, peer), device_id_type=pl.DeviceIdType.MESH
        )
    for peer in prompt_peers:
        pl.semaphore_signal(
            barrier, inc=1, device_id=(peer, me), device_id_type=pl.DeviceIdType.MESH
        )

    own_block = pl.ds(pl.multiple_of(me * block, 16), block)
    loads = [
        pltpu.make_async_copy(kv_hbm.at[0], win.at[pl.ds(rows, rows)], in_sem.at[0]),
        pltpu.make_async_copy(pkv_hbm.at[0], pfx.at[own_block], in_sem.at[1]),
        pltpu.make_async_copy(q_hbm.at[0], q_ref, in_sem.at[2]),
        pltpu.make_async_copy(up_hbm.at[0], up_ref, in_sem.at[3]),
    ]
    for load in loads:
        load.start()

    total = lens_ref[0, 0]
    for r in range(1, responses):
        total = total + lens_ref[0, r]
    lens_all[my_p] = jnp.full((8, 128), total, jnp.int32).astype(F32)

    pl.semaphore_wait(barrier, n_seq - 1 + n_prompt - 1)

    def remote(src, dst, send, recv, target):
        return pltpu.make_async_remote_copy(
            src_ref=src,
            dst_ref=dst,
            send_sem=send,
            recv_sem=recv,
            device_id=target,
            device_id_type=pl.DeviceIdType.MESH,
        )

    def part(j):
        return pl.ds(j * TILE, TILE)

    def prev_copy(j):
        return remote(
            kv_hbm.at[0, part(j)],
            win.at[part(j)],
            prev_send.at[j],
            prev_recv.at[j],
            (my_p, me + 1),
        )

    def ret_copy(j):
        return remote(
            ret_out.at[part(j)],
            ret_in.at[part(j)],
            ret_send.at[j],
            ret_recv.at[j],
            (my_p, me - 1),
        )

    def pf_copy(d, sender, target):
        rows_of = pl.ds(pl.multiple_of(sender * block, 16), block)
        return remote(
            pkv_hbm.at[0], pfx.at[rows_of], pf_send.at[d], pf_recv.at[sender], (my_p, target)
        )

    def len_copy(d, sender, target):
        return remote(
            lens_all.at[sender],
            lens_all.at[sender],
            len_send.at[d],
            len_recv.at[sender],
            (target, me),
        )

    def gp_copy(d, sender, target):
        rows_of = pl.ds(pl.multiple_of(target * block, 16), block)
        return remote(
            gp_out.at[rows_of],
            gp_in.at[sender],
            gp_send.at[d],
            gp_recv.at[sender],
            (my_p, target),
        )

    order = [tiles - 1] + list(range(tiles - 1))
    for d, peer in enumerate(seq_peers):
        pf_copy(d, me, peer).start()

    @pl.when(has_next)
    def _():
        prev_copy(order[0]).start()

    for d, peer in enumerate(prompt_peers):
        len_copy(d, my_p, peer).start()

    @pl.when(has_next)
    def _():
        for j in order[1:]:
            prev_copy(j).start()

    @pl.when(jnp.logical_not(has_prev))
    def _():
        win[pl.ds(0, rows)] = jnp.zeros((rows, 2 * dim), BF16)

    @pl.when(jnp.logical_not(has_next))
    def _():
        ret_in[...] = jnp.zeros((rows, 2 * dim), BF16)

    acc[...] = jnp.zeros_like(acc)
    acc_p[...] = jnp.zeros_like(acc_p)
    win_vt[pl.ds(dim, ONES)] = jnp.ones((ONES, 2 * rows), BF16)
    pfx_vt[pl.ds(dim, ONES)] = jnp.ones((ONES, pfx.shape[0]), BF16)

    def turn(j):
        keys = win[part(j), :dim]
        values = win[part(j), dim:]
        win_kt[:, part(j)] = keys.T
        win_vt[pl.ds(0, dim), part(j)] = values.T

    loads[0].wait()
    for j in range(tiles, 2 * tiles):
        turn(j)
    for load in loads[1:]:
        load.wait()
    for d, peer in enumerate(seq_peers):
        pf_copy(d, peer, me).wait_recv()
    pfx_kt[...] = pfx[:, :dim].T
    pfx_vt[pl.ds(0, dim)] = pfx[:, dim:].T

    @pl.when(has_prev)
    def _():
        prev_copy(order[0]).wait_recv()

    turn(order[0])
    for d, peer in enumerate(prompt_peers):
        len_copy(d, peer, my_p).wait_recv()
    tokens = lens_all[0]
    for p in range(1, n_prompt):
        tokens = tokens + lens_all[p]
    factor = (F32(n_prompt * n_seq * rows) / tokens)[:1]
    factor2 = jnp.concatenate([factor] * PAIR, axis=1)

    def out_copies(i):
        return (
            pltpu.make_async_copy(
                att.at[part(i)], att_hbm.at[0, part(i)], out_sem.at[2 * i]
            ),
            pltpu.make_async_copy(
                gq.at[part(i)], gq_hbm.at[0, part(i)], out_sem.at[2 * i + 1]
            ),
        )

    def tile_step(i):
        start_row = pl.multiple_of(i * TILE, TILE)
        own = pl.ds(start_row, TILE)
        window = pl.ds(start_row, span)

        slots = me * rows + start_row + lax.broadcasted_iota(jnp.int32, (1, TILE), 1)
        first = jnp.zeros((1, TILE), jnp.int32)
        end = jnp.int32(0)
        for r in range(responses):
            end = end + lens_ref[0, r]
            first = jnp.where(slots >= end, end, first)
        live = jnp.where(slots < end, F32(1), F32(0))
        live2 = jnp.concatenate([live] * PAIR, axis=1)
        key_slots = (me - 1) * rows + start_row + lax.broadcasted_iota(jnp.int32, (span, TILE), 0)
        seen = (key_slots >= first) & (key_slots <= slots)
        one_bias = jnp.where(seen, F32(0), F32(HIDDEN))
        for k in range(PAIR):
            bias[:, pl.ds(k * TILE, TILE)] = one_bias

        k_w = win[window, :dim]
        v_w = win[window, dim:]
        k_p = pfx[:, :dim]
        v_p = pfx[:, dim:]
        kt_w = win_kt[:, window]
        vt_w = win_vt[:, window]

        q_parts, g_parts = [], []
        wp_parts, ww_parts, sp_parts, sw_parts = [], [], [], []
        for pair in range(heads // PAIR):
            cols = [pl.ds((pair * PAIR + k) * dim, dim) for k in range(PAIR)]
            q2 = jnp.concatenate([q_ref[own, c] for c in cols], axis=0)
            up_t = jnp.concatenate([up_ref[own, c].T for c in cols], axis=1)
            s_p = mm_nt(k_p, q2)
            s_w = mm_nt(k_w, q2) + bias[...]
            top = jnp.maximum(
                jnp.max(s_p, axis=0, keepdims=True), jnp.max(s_w, axis=0, keepdims=True)
            )
            step = scale * math.log2(math.e)
            w_p = jnp.exp2((s_p - top) * step).astype(BF16)
            w_w = jnp.exp2((s_w - top) * step).astype(BF16)
            mixed = mm(pfx_vt[...], w_p) + mm(vt_w, w_w)
            inverse = live2 / mixed[dim : dim + 1]
            att_t = (mixed[:dim] * inverse).astype(BF16)
            g_t = (up_t.astype(F32) * inverse).astype(BF16)
            delta = jnp.sum(g_t.astype(F32) * att_t.astype(F32), axis=0, keepdims=True)
            d_p = (w_p.astype(F32) * (mm(v_p, g_t) - delta)).astype(BF16)
            d_w = (w_w.astype(F32) * (mm(v_w, g_t) - delta)).astype(BF16)
            gq_t = ((mm(pfx_kt[...], d_p) + mm(kt_w, d_w)) * (factor2 * scale)).astype(BF16)
            for k, c in enumerate(cols):
                att[own, c] = att_t[:, k * TILE : (k + 1) * TILE].T
                gq[own, c] = gq_t[:, k * TILE : (k + 1) * TILE].T
            q_parts.append(q2)
            g_parts.append(g_t)
            wp_parts.append(w_p)
            ww_parts.append(w_w)
            sp_parts.append(d_p)
            sw_parts.append(d_w)
        q_all = jnp.concatenate(q_parts, axis=0)
        g_all = jnp.concatenate(g_parts, axis=1)
        acc_p[:, :dim] += mm(jnp.concatenate(sp_parts, axis=1), q_all)
        acc[window, :dim] += mm(jnp.concatenate(sw_parts, axis=1), q_all)
        acc_p[:, dim:] += mm_nt(jnp.concatenate(wp_parts, axis=1), g_all)
        acc[window, dim:] += mm_nt(jnp.concatenate(ww_parts, axis=1), g_all)

    def give_back(j):
        ret_out[part(j)] = acc[part(j)].astype(BF16)

        @pl.when(has_prev)
        def _():
            ret_copy(j).start()

    def round_step(s, carry):
        i = lax.rem(s + tiles - 1, tiles)

        @pl.when(s == 1)
        def _():
            @pl.when(has_prev)
            def _():
                for j in order[1:]:
                    prev_copy(j).wait_recv()

            for j in order[1:]:
                turn(j)

        tile_step(i)
        for copy in out_copies(i):
            copy.start()
        for k in range(1, tiles - 1):

            @pl.when(s == k)
            def _():
                give_back(k - 1)

        return carry

    lax.fori_loop(0, tiles, round_step, 0)

    gp_out[...] = acc_p[...].astype(BF16)
    for d, peer in enumerate(seq_peers):
        gp_copy(d, me, peer).start()
    for j in (tiles - 2, tiles - 1):
        give_back(j)

    final = jnp.concatenate([factor * scale, factor], axis=1)
    for j in range(tiles):

        @pl.when(has_next)
        def _():
            pltpu.make_async_remote_copy(
                src_ref=ret_out.at[part(j)],
                dst_ref=ret_in.at[part(j)],
                send_sem=ret_send.at[j],
                recv_sem=ret_recv.at[j],
                device_id=(my_p, me + 1),
                device_id_type=pl.DeviceIdType.MESH,
            ).wait_recv()

        gkv[part(j)] = (acc[part(tiles + j)] + ret_in[part(j)].astype(F32)) * final
    gkv_copy = pltpu.make_async_copy(gkv, gkv_hbm.at[0], out_sem.at[2 * tiles])
    gkv_copy.start()

    sums = acc_p[own_block]
    for d, peer in enumerate(seq_peers):
        gp_copy(d, peer, me).wait_recv()
        sums = sums + gp_in[peer].astype(F32)
    gpf[...] = sums * final
    gpf_copy = pltpu.make_async_copy(gpf, gpf_hbm.at[0], out_sem.at[2 * tiles + 1])
    gpf_copy.start()

    for d, peer in enumerate(seq_peers):
        pf_copy(d, me, peer).wait_send()
        gp_copy(d, me, peer).wait_send()
    for d, peer in enumerate(prompt_peers):
        len_copy(d, my_p, peer).wait_send()

    @pl.when(has_next)
    def _():
        for j in order:
            prev_copy(j).wait_send()

    @pl.when(has_prev)
    def _():
        for j in range(tiles):
            ret_copy(j).wait_send()

    for i in range(tiles):
        for copy in out_copies(i):
            copy.wait()
    gkv_copy.wait()
    gpf_copy.wait()


def body(n_prompt, n_seq, queries, resp_kv, prefix_kv, lengths, upstream):
    rows, width = queries.shape[1:]
    dim = resp_kv.shape[2] // 2
    block = prefix_kv.shape[1]
    prefix = block * n_seq
    tiles = rows // TILE
    dma = pltpu.SemaphoreType.DMA
    anywhere = pl.BlockSpec(memory_space=pl.ANY)
    vmem = pltpu.VMEM
    return pl.pallas_call(
        functools.partial(kernel, n_prompt, n_seq),
        out_shape=(
            jax.ShapeDtypeStruct(queries.shape, BF16),
            jax.ShapeDtypeStruct(queries.shape, BF16),
            jax.ShapeDtypeStruct(resp_kv.shape, F32),
            jax.ShapeDtypeStruct(prefix_kv.shape, F32),
        ),
        in_specs=[pl.BlockSpec(memory_space=pltpu.SMEM)] + [anywhere] * 4,
        out_specs=(anywhere,) * 4,
        scratch_shapes=[
            vmem((rows, width), BF16),
            vmem((rows, width), BF16),
            vmem((2 * rows, 2 * dim), BF16),
            vmem((prefix, 2 * dim), BF16),
            vmem((dim, 2 * rows), BF16),
            vmem((dim + ONES, 2 * rows), BF16),
            vmem((dim, prefix), BF16),
            vmem((dim + ONES, prefix), BF16),
            vmem((rows + TILE, PAIR * TILE), F32),
            vmem((rows, width), BF16),
            vmem((rows, width), BF16),
            vmem((2 * rows, 2 * dim), F32),
            vmem((prefix, 2 * dim), F32),
            vmem((rows, 2 * dim), BF16),
            vmem((rows, 2 * dim), BF16),
            vmem((prefix, 2 * dim), BF16),
            vmem((n_seq, block, 2 * dim), BF16),
            vmem((rows, 2 * dim), F32),
            vmem((block, 2 * dim), F32),
            vmem((n_prompt, 8, 128), F32),
            dma((4,)),
            dma((2 * tiles + 2,)),
            dma((n_seq,)),
            dma((n_seq,)),
            dma((tiles,)),
            dma((tiles,)),
            dma((n_prompt,)),
            dma((n_prompt,)),
            dma((tiles,)),
            dma((tiles,)),
            dma((n_seq,)),
            dma((n_seq,)),
        ],
        compiler_params=pltpu.CompilerParams(
            collective_id=0, has_side_effects=True, vmem_limit_bytes=50 * 1024 * 1024
        ),
        name="attention_core",
    )(lengths, queries, resp_kv, prefix_kv, upstream)


def solution(mesh):
    spec = P("prompt", "seq", None)
    return jax.shard_map(
        functools.partial(body, mesh.shape["prompt"], mesh.shape["seq"]),
        mesh=mesh,
        in_specs=(spec, spec, spec, P("prompt", None), spec),
        out_specs=(spec, spec, spec, spec),
        check_vma=False,
    )
```

time: 110 us -> 42.7 us (0.39); the launches traced: 109 us -> 42.5 us
  Pallas kernels: 0 us -> 34.9 us
  matrix products: 31.1 us -> 0 us
  blocking collectives: 26 us -> 0 us
  between operations: 15.9 us -> 0.65 us
  other arithmetic: 11.2 us -> 0 us
  waiting for transfers between devices: 9.57 us -> 0 us
  starting transfers between devices: 6.79 us -> 0 us
    pallas_call x0 -> x1, Pallas kernels: none -> 34.9 us  [body(): pl.pallas_call(functools.partial(kernel, n_prompt, n_seq), out_shape=(jax...]
    dot_general x48 -> x0, matrix products: 31.1 us -> none  [the longest x8 9.74 us: block_terms(): jnp.einsum('rgk,kd->rgd', dscores, key_part, preferred_element_type=jnp.f...]
    psum x1 -> x0, blocking collectives: 18.4 us -> none  [body(): live_total = lax.psum(jnp.sum(lengths[0]).astype(jnp.float32), 'prompt')]
    all_gather x1 -> x0, blocking collectives: 7.65 us -> none  [body(): prefix_all = lax.all_gather(prefix_kv[0], 'seq', axis=0, tiled=True)]
    reduce_scatter x1 -> x0, waiting for transfers between devices: 7.15 us -> none  [body(): lax.psum_scatter(kv_grads[:prefix_len], 'seq', scatter_dimension=0, tiled...]
    ppermute x2 -> x0, starting transfers between devices: 6.75 us -> none  [shifted(): return lax.ppermute(block, axis, route)]
    reduce_sum x11 -> x0, other arithmetic: 5.01 us -> none  [the longest x8 3.31 us: block_terms(): row_total = jnp.sum(weights, axis=-1, keepdims=True)]
    ppermute x2 -> x0, waiting for transfers between devices: 2.41 us -> none  [shifted(): return lax.ppermute(block, axis, route)]
  transfers between devices with their start and end apart: 3 -> 0, of which waited for: 2 -> 0; matrix products, arithmetic and copies ran while one was open for 12% -> 0% of each run, Pallas kernels for 0% -> 0%
where the time goes in v1:
time: 42.7 us; the launch traced here: 42.5 us
  Pallas kernels  34.9 us (82%)
  local copies, waits for them, and re-layouts  6.91 us (16%)
  between operations  0.65 us (2%)
    pallas_call x1, Pallas kernels, body(): pl.pallas_call(functools.partial(kernel, n_prompt, n_seq), out_shape=(jax...  34.9 us
    unnamed x12, local copies, waits for them, and re-layouts  6.91 us

profile of v1, /device:TPU:1, one launch (start us, length us, event | category | flops | bytes accessed | tf_op | source)
XLA Modules:
  0.0 42.5 jit_solution(536574515859990451)
XLA Ops:
  0.6 0.0 copy-start
  0.6 1.2 %copy-done = bf16[1,512,1024]{2,1,0:T(8,128)(2,1)S(1)} copy-done((bf16[1,512,1024]{2,1,0:T(8,128)(2,1)S(1)}, bf16[1,512,1024]{2,1,0:T(8,128)(2,1)}, u32[]{:S(2)}) %copy-start) | copy-done | bytes 1048600
  1.9 0.0 copy-start.1
  1.9 0.9 %copy-done.1 = bf16[1,512,256]{2,1,0:T(8,128)(2,1)S(1)} copy-done((bf16[1,512,256]{2,1,0:T(8,128)(2,1)S(1)}, bf16[1,512,256]{2,1,0:T(8,128)(2,1)}, u32[]{:S(2)}) %copy-start.1) | copy-done | bytes 262168
  2.8 0.0 copy-start.2
  2.8 0.7 %copy-done.2 = bf16[1,48,256]{2,1,0:T(8,128)(2,1)S(1)} copy-done((bf16[1,48,256]{2,1,0:T(8,128)(2,1)S(1)}, bf16[1,48,256]{2,1,0:T(8,128)(2,1)}, u32[]{:S(2)}) %copy-start.2) | copy-done | bytes 24600
  3.5 0.0 copy-start.3
  3.5 0.7 %copy-done.3 = s32[1,4]{1,0:T(1,128)S(1)} copy-done((s32[1,4]{1,0:T(1,128)S(1)}, s32[1,4]{1,0:T(1,128)}, u32[]{:S(2)}) %copy-start.3) | copy-done | bytes 40
  4.2 34.9 %attention_core.1 = (bf16[1,512,1024]{2,1,0:T(8,128)(2,1)S(1)}, bf16[1,512,1024]{2,1,0:T(8,128)(2,1)S(1)}, f32[1,512,256]{2,1,0:T(8,128)S(1)}, f32[1,48,256]{2,1,0:T(8,128)S(1)}) custom-call(s32[1,4]{1,0:T(1,128)S(1)} %copy-done.3, bf16[1,512,1024]{2,1,0:T(8,128)(2,1)S(1)} %copy-done, bf16[1,512,256]{2,1,0:T(8,128)(2,1)S(1)} %copy-done.1, ...), custom_call_target="tpu_custom_call" | custom-call | tf_op jit(solution)/shard_map/attention_core/pallas_call | solution.py:400
  39.1 1.0 %copy.13 = bf16[1,512,1024]{2,1,0:T(8,128)(2,1)} copy(bf16[1,512,1024]{2,1,0:T(8,128)(2,1)S(1)} %get-tuple-element.8) | data formatting | bytes 2097152
  40.1 1.0 %copy.14 = bf16[1,512,1024]{2,1,0:T(8,128)(2,1)} copy(bf16[1,512,1024]{2,1,0:T(8,128)(2,1)S(1)} %get-tuple-element.9) | data formatting | bytes 2097152
  41.1 0.8 %copy.15 = f32[1,512,256]{2,1,0:T(8,128)} copy(f32[1,512,256]{2,1,0:T(8,128)S(1)} %get-tuple-element.10) | data formatting | bytes 1048576
  41.9 0.6 %copy.16 = f32[1,48,256]{2,1,0:T(8,128)} copy(f32[1,48,256]{2,1,0:T(8,128)S(1)} %get-tuple-element.11) | data formatting | bytes 98304
Async XLA Ops:
  0.6 1.2 %copy-start = (bf16[1,512,1024]{2,1,0:T(8,128)(2,1)S(1)}, bf16[1,512,1024]{2,1,0:T(8,128)(2,1)}, u32[]{:S(2)}) copy-start(bf16[1,512,1024]{2,1,0:T(8,128)(2,1)} %q_hbm.1) | copy-start | bytes 3145732
  1.9 0.9 %copy-start.1 = (bf16[1,512,256]{2,1,0:T(8,128)(2,1)S(1)}, bf16[1,512,256]{2,1,0:T(8,128)(2,1)}, u32[]{:S(2)}) copy-start(bf16[1,512,256]{2,1,0:T(8,128)(2,1)} %kv_hbm.1) | copy-start | bytes 786436
  2.8 0.7 %copy-start.2 = (bf16[1,48,256]{2,1,0:T(8,128)(2,1)S(1)}, bf16[1,48,256]{2,1,0:T(8,128)(2,1)}, u32[]{:S(2)}) copy-start(bf16[1,48,256]{2,1,0:T(8,128)(2,1)} %pkv_hbm.1) | copy-start | bytes 73732
  3.5 0.7 %copy-start.3 = (s32[1,4]{1,0:T(1,128)S(1)}, s32[1,4]{1,0:T(1,128)}, u32[]{:S(2)}) copy-start(s32[1,4]{1,0:T(1,128)} %lens_ref.1) | copy-start | bytes 52

commit v2 on v1

--- a/solution.py
+++ b/solution.py
@@ -45,6 +45,9 @@
     pfx_kt,
     pfx_vt,
     bias,
+    s_ref,
+    w_ref,
+    d_ref,
     att,
     gq,
     acc,
@@ -74,6 +77,7 @@
     heads = q_ref.shape[1] // dim
     tiles = rows // TILE
     block = pkv_hbm.shape[1]
+    prefix = pfx.shape[0]
     span = rows + TILE
     responses = lens_ref.shape[1]
     scale = dim ** (-0.5)
@@ -251,54 +255,117 @@
         live2 = jnp.concatenate([live] * PAIR, axis=1)
         key_slots = (me - 1) * rows + start_row + lax.broadcasted_iota(jnp.int32, (span, TILE), 0)
         seen = (key_slots >= first) & (key_slots <= slots)
-        one_bias = jnp.where(seen, F32(0), F32(HIDDEN))
-        for k in range(PAIR):
-            bias[:, pl.ds(k * TILE, TILE)] = one_bias
-
-        k_w = win[window, :dim]
-        v_w = win[window, dim:]
-        k_p = pfx[:, :dim]
-        v_p = pfx[:, dim:]
-        kt_w = win_kt[:, window]
-        vt_w = win_vt[:, window]
-
-        q_parts, g_parts = [], []
-        wp_parts, ww_parts, sp_parts, sw_parts = [], [], [], []
-        for pair in range(heads // PAIR):
-            cols = [pl.ds((pair * PAIR + k) * dim, dim) for k in range(PAIR)]
-            q2 = jnp.concatenate([q_ref[own, c] for c in cols], axis=0)
-            up_t = jnp.concatenate([up_ref[own, c].T for c in cols], axis=1)
-            s_p = mm_nt(k_p, q2)
-            s_w = mm_nt(k_w, q2) + bias[...]
-            top = jnp.maximum(
-                jnp.max(s_p, axis=0, keepdims=True), jnp.max(s_w, axis=0, keepdims=True)
+        bias[...] = jnp.where(seen, F32(0), F32(HIDDEN))
+
+        q_of, top_of, g_of, delta_of = {}, {}, {}, {}
+        pairs = heads // PAIR
+        width = PAIR * TILE
+        chunks = [(pfx, pl.ds(lo, min(TILE, prefix - lo)), pl.ds(lo, min(TILE, prefix - lo)), None)
+                  for lo in range(0, prefix, TILE)]
+        chunks += [
+            (
+                win,
+                pl.ds(pl.multiple_of(start_row + lo, TILE), TILE),
+                pl.ds(prefix + lo, TILE),
+                pl.ds(lo, TILE),
             )
+            for lo in range(0, span, TILE)
+        ]
+
+        def cols_of(pair):
+            return [pl.ds((pair * PAIR + k) * dim, dim) for k in range(PAIR)]
+
+        def score_stage(pair):
+            def begin():
+                q_of[pair] = jnp.concatenate([q_ref[own, c] for c in cols_of(pair)], axis=0)
+                top_of[pair] = []
+
+            def chunk(source, keys, at, mask_rows):
+                s = mm_nt(source[keys, :dim], q_of[pair])
+                if mask_rows is not None:
+                    hide = bias[mask_rows]
+                    s = s + jnp.concatenate([hide] * PAIR, axis=1)
+                s_ref[pair % 2, at] = s
+                top_of[pair].append(jnp.max(s.reshape(-1, 8, width), axis=0))
+
+            def end():
+                top_of[pair] = jnp.max(
+                    functools.reduce(jnp.maximum, top_of[pair]), axis=0, keepdims=True
+                )
+
+            return begin, chunk, end
+
+        def weight_stage(pair):
             step = scale * math.log2(math.e)
-            w_p = jnp.exp2((s_p - top) * step).astype(BF16)
-            w_w = jnp.exp2((s_w - top) * step).astype(BF16)
-            mixed = mm(pfx_vt[...], w_p) + mm(vt_w, w_w)
-            inverse = live2 / mixed[dim : dim + 1]
-            att_t = (mixed[:dim] * inverse).astype(BF16)
-            g_t = (up_t.astype(F32) * inverse).astype(BF16)
-            delta = jnp.sum(g_t.astype(F32) * att_t.astype(F32), axis=0, keepdims=True)
-            d_p = (w_p.astype(F32) * (mm(v_p, g_t) - delta)).astype(BF16)
-            d_w = (w_w.astype(F32) * (mm(v_w, g_t) - delta)).astype(BF16)
-            gq_t = ((mm(pfx_kt[...], d_p) + mm(kt_w, d_w)) * (factor2 * scale)).astype(BF16)
-            for k, c in enumerate(cols):
-                att[own, c] = att_t[:, k * TILE : (k + 1) * TILE].T
-                gq[own, c] = gq_t[:, k * TILE : (k + 1) * TILE].T
-            q_parts.append(q2)
-            g_parts.append(g_t)
-            wp_parts.append(w_p)
-            ww_parts.append(w_w)
-            sp_parts.append(d_p)
-            sw_parts.append(d_w)
-        q_all = jnp.concatenate(q_parts, axis=0)
-        g_all = jnp.concatenate(g_parts, axis=1)
-        acc_p[:, :dim] += mm(jnp.concatenate(sp_parts, axis=1), q_all)
-        acc[window, :dim] += mm(jnp.concatenate(sw_parts, axis=1), q_all)
-        acc_p[:, dim:] += mm_nt(jnp.concatenate(wp_parts, axis=1), g_all)
-        acc[window, dim:] += mm_nt(jnp.concatenate(ww_parts, axis=1), g_all)
+            lanes = pl.ds(pair * width, width)
+
+            def begin():
+                pass
+
+            def chunk(source, keys, at, mask_rows):
+                w_ref[at, lanes] = jnp.exp2((s_ref[pair % 2, at] - top_of[pair]) * step).astype(
+                    BF16
+                )
+
+            def end():
+                mixed = mm(pfx_vt[...], w_ref[pl.ds(0, prefix), lanes])
+                mixed = mixed + mm(win_vt[:, window], w_ref[pl.ds(prefix, span), lanes])
+                inverse = live2 / mixed[dim : dim + 1]
+                att_t = (mixed[:dim] * inverse).astype(BF16)
+                up_t = jnp.concatenate([up_ref[own, c].T for c in cols_of(pair)], axis=1)
+                g_t = (up_t.astype(F32) * inverse).astype(BF16)
+                g_of[pair] = g_t
+                delta_of[pair] = jnp.sum(
+                    g_t.astype(F32) * att_t.astype(F32), axis=0, keepdims=True
+                )
+                for k, c in enumerate(cols_of(pair)):
+                    att[own, c] = att_t[:, k * TILE : (k + 1) * TILE].T
+
+            return begin, chunk, end
+
+        def grad_stage(pair):
+            lanes = pl.ds(pair * width, width)
+
+            def begin():
+                pass
+
+            def chunk(source, keys, at, mask_rows):
+                dp = mm(source[keys, dim:], g_of[pair]) - delta_of[pair]
+                d_ref[at, lanes] = (w_ref[at, lanes].astype(F32) * dp).astype(BF16)
+
+            def end():
+                gq_t = mm(pfx_kt[...], d_ref[pl.ds(0, prefix), lanes])
+                gq_t = gq_t + mm(win_kt[:, window], d_ref[pl.ds(prefix, span), lanes])
+                gq_t = (gq_t * (factor2 * scale)).astype(BF16)
+                for k, c in enumerate(cols_of(pair)):
+                    gq[own, c] = gq_t[:, k * TILE : (k + 1) * TILE].T
+                if pair % 2 == 1:
+                    both = pl.ds((pair - 1) * width, 2 * width)
+                    q_all = jnp.concatenate([q_of[pair - 1], q_of[pair]], axis=0)
+                    g_all = jnp.concatenate([g_of[pair - 1], g_of[pair]], axis=1)
+                    top_rows, low_rows = pl.ds(0, prefix), pl.ds(prefix, span)
+                    acc_p[:, :dim] += mm(d_ref[top_rows, both], q_all)
+                    acc[window, :dim] += mm(d_ref[low_rows, both], q_all)
+                    acc_p[:, dim:] += mm_nt(w_ref[top_rows, both], g_all)
+                    acc[window, dim:] += mm_nt(w_ref[low_rows, both], g_all)
+
+            return begin, chunk, end
+
+        for t in range(pairs + 2):
+            running = []
+            if t < pairs:
+                running.append(score_stage(t))
+            if 0 <= t - 1 < pairs:
+                running.append(weight_stage(t - 1))
+            if 0 <= t - 2 < pairs:
+                running.append(grad_stage(t - 2))
+            for begin, _, _ in running:
+                begin()
+            for each in chunks:
+                for _, chunk, _ in running:
+                    chunk(*each)
+            for _, _, end in running:
+                end()
 
     def give_back(j):
         ret_out[part(j)] = acc[part(j)].astype(BF16)
@@ -388,6 +455,24 @@
     gpf_copy.wait()
 
 
+def hand_over(*refs):
+    half = (len(refs) - 1) // 2
+    sources, targets, sems = refs[:half], refs[half : 2 * half], refs[-1]
+    copies = []
+    for a, (source, target) in enumerate(zip(sources, targets)):
+        pieces = 4 if source.shape[1] % 64 == 0 else 1
+        step = source.shape[1] // pieces
+        for p in range(pieces):
+            rows = pl.ds(p * step, step)
+            copies.append(
+                pltpu.make_async_copy(source.at[0, rows], target.at[0, rows], sems.at[a, p])
+            )
+    for copy in copies:
+        copy.start()
+    for copy in copies:
+        copy.wait()
+
+
 def body(n_prompt, n_seq, queries, resp_kv, prefix_kv, lengths, upstream):
     rows, width = queries.shape[1:]
     dim = resp_kv.shape[2] // 2
@@ -397,14 +482,15 @@
     dma = pltpu.SemaphoreType.DMA
     anywhere = pl.BlockSpec(memory_space=pl.ANY)
     vmem = pltpu.VMEM
-    return pl.pallas_call(
+    out_shape = (
+        jax.ShapeDtypeStruct(queries.shape, BF16),
+        jax.ShapeDtypeStruct(queries.shape, BF16),
+        jax.ShapeDtypeStruct(resp_kv.shape, F32),
+        jax.ShapeDtypeStruct(prefix_kv.shape, F32),
+    )
+    results = pl.pallas_call(
         functools.partial(kernel, n_prompt, n_seq),
-        out_shape=(
-            jax.ShapeDtypeStruct(queries.shape, BF16),
-            jax.ShapeDtypeStruct(queries.shape, BF16),
-            jax.ShapeDtypeStruct(resp_kv.shape, F32),
-            jax.ShapeDtypeStruct(prefix_kv.shape, F32),
-        ),
+        out_shape=out_shape,
         in_specs=[pl.BlockSpec(memory_space=pltpu.SMEM)] + [anywhere] * 4,
         out_specs=(anywhere,) * 4,
         scratch_shapes=[
@@ -416,7 +502,10 @@
             vmem((dim + ONES, 2 * rows), BF16),
             vmem((dim, prefix), BF16),
             vmem((dim + ONES, prefix), BF16),
-            vmem((rows + TILE, PAIR * TILE), F32),
+            vmem((rows + TILE, TILE), F32),
+            vmem((2, prefix + rows + TILE, PAIR * TILE), F32),
+            vmem((prefix + rows + TILE, width), BF16),
+            vmem((prefix + rows + TILE, width), BF16),
             vmem((rows, width), BF16),
             vmem((rows, width), BF16),
             vmem((2 * rows, 2 * dim), F32),
@@ -442,10 +531,18 @@
             dma((n_seq,)),
         ],
         compiler_params=pltpu.CompilerParams(
-            collective_id=0, has_side_effects=True, vmem_limit_bytes=50 * 1024 * 1024
+            collective_id=0, has_side_effects=True, vmem_limit_bytes=62 * 1024 * 1024
         ),
         name="attention_core",
     )(lengths, queries, resp_kv, prefix_kv, upstream)
+    return pl.pallas_call(
+        hand_over,
+        out_shape=out_shape,
+        in_specs=[anywhere] * 4,
+        out_specs=(anywhere,) * 4,
+        scratch_shapes=[dma((4, 4))],
+        name="hand_over",
+    )(*results)
 
 
 def solution(mesh):

time: 42.7 us -> 114 us (2.67)
  Pallas kernels: 34.9 us -> 113 us
  local copies, waits for them, and re-layouts: 6.91 us -> 0 us
    pallas_call x1 -> x2, Pallas kernels: 34.9 us -> 113 us  [the longest x1 82.1 us: body(): pl.pallas_call(hand_over, out_shape=out_shape, in_specs=[anywhere] * 4, o...]
    unnamed x12 -> x0, local copies, waits for them, and re-layouts: 6.91 us -> none
where the time goes in v2:
time: 114 us
  Pallas kernels  113 us (99%)
    pallas_call x1, Pallas kernels, body(): pl.pallas_call(hand_over, out_shape=out_shape, in_specs=[anywhere] * 4, o...  82.1 us
    pallas_call x1, Pallas kernels, body(): pl.pallas_call(functools.partial(kernel, n_prompt, n_seq), out_shape=out_...  30.9 us

profile of v2, /device:TPU:1, one launch (start us, length us, event | category | flops | bytes accessed | tf_op | source)
XLA Modules:
  0.0 113.7 jit_solution(15229582884929910634)
XLA Ops:
  0.6 30.9 %attention_core.1 = (bf16[1,512,1024]{2,1,0:T(8,128)(2,1)}, bf16[1,512,1024]{2,1,0:T(8,128)(2,1)}, f32[1,512,256]{2,1,0:T(8,128)}, f32[1,48,256]{2,1,0:T(8,128)}) custom-call(s32[1,4]{1,0:T(1,128)} %lens_ref.1, bf16[1,512,1024]{2,1,0:T(8,128)(2,1)} %q_hbm.1, bf16[1,512,256]{2,1,0:T(8,128)(2,1)} %kv_hbm.1, bf16[1,48,256]{2,1,0:T(8,128)(2,1)} %pkv_hbm.1, ...), custom_call_target="tpu_custom_call" | custom-call | tf_op jit(solution)/shard_map/attention_core/pallas_call | solution.py:491
  31.6 82.1 %hand_over.1 = (bf16[1,512,1024]{2,1,0:T(8,128)(2,1)}, bf16[1,512,1024]{2,1,0:T(8,128)(2,1)}, f32[1,512,256]{2,1,0:T(8,128)}, f32[1,48,256]{2,1,0:T(8,128)}) custom-call(bf16[1,512,1024]{2,1,0:T(8,128)(2,1)} %get-tuple-element.8.refs_0_, bf16[1,512,1024]{2,1,0:T(8,128)(2,1)} %get-tuple-element.9.refs_1_, f32[1,512,256]{2,1,0:T(8,128)} %get-tuple-element.10.refs_2_, ...), custom_call_target="tpu_custom_call" | custom-call | tf_op jit(solution)/shard_map/hand_over/pallas_call | solution.py:538

commit v3 on v1

--- a/solution.py
+++ b/solution.py
@@ -45,6 +45,12 @@
     pfx_kt,
     pfx_vt,
     bias,
+    s_ref,
+    top_ref,
+    w_ref,
+    g_ref,
+    delta_ref,
+    d_ref,
     att,
     gq,
     acc,
@@ -58,6 +64,7 @@
     lens_all,
     in_sem,
     out_sem,
+    last_sem,
     pf_send,
     pf_recv,
     prev_send,
@@ -69,11 +76,11 @@
     gp_send,
     gp_recv,
 ):
-    rows = q_ref.shape[0]
+    pairs, rows, width = q_ref.shape
     dim = win.shape[1] // 2
-    heads = q_ref.shape[1] // dim
     tiles = rows // TILE
     block = pkv_hbm.shape[1]
+    prefix = pfx.shape[0]
     span = rows + TILE
     responses = lens_ref.shape[1]
     scale = dim ** (-0.5)
@@ -99,11 +106,25 @@
     loads = [
         pltpu.make_async_copy(kv_hbm.at[0], win.at[pl.ds(rows, rows)], in_sem.at[0]),
         pltpu.make_async_copy(pkv_hbm.at[0], pfx.at[own_block], in_sem.at[1]),
-        pltpu.make_async_copy(q_hbm.at[0], q_ref, in_sem.at[2]),
-        pltpu.make_async_copy(up_hbm.at[0], up_ref, in_sem.at[3]),
     ]
+    for pair in range(pairs):
+        lanes = pl.ds(pair * width, width)
+        for k, (source, target) in enumerate(((q_hbm, q_ref), (up_hbm, up_ref))):
+            loads.append(
+                pltpu.make_async_copy(
+                    source.at[0, :, lanes], target.at[pair], in_sem.at[2 + 2 * pair + k]
+                )
+            )
     for load in loads:
         load.start()
+
+    s_ref[1] = jnp.zeros(s_ref.shape[1:], F32)
+    top_ref[1] = jnp.zeros(top_ref.shape[1:], F32)
+    for slot in (1, 2):
+        w_ref[slot] = jnp.zeros(w_ref.shape[1:], BF16)
+        g_ref[slot] = jnp.zeros(g_ref.shape[1:], BF16)
+    delta_ref[0] = jnp.zeros(delta_ref.shape[1:], F32)
+    d_ref[1] = jnp.zeros(d_ref.shape[1:], BF16)
 
     total = lens_ref[0, 0]
     for r in range(1, responses):
@@ -226,79 +247,121 @@
     factor = (F32(n_prompt * n_seq * rows) / tokens)[:1]
     factor2 = jnp.concatenate([factor] * PAIR, axis=1)
 
+    ends = []
+    for r in range(responses):
+        ends.append(lens_ref[0, r] + (ends[-1] if ends else 0))
+    units = tiles * pairs
+    step_scale = scale * math.log2(math.e)
+
     def out_copies(i):
-        return (
-            pltpu.make_async_copy(
-                att.at[part(i)], att_hbm.at[0, part(i)], out_sem.at[2 * i]
-            ),
-            pltpu.make_async_copy(
-                gq.at[part(i)], gq_hbm.at[0, part(i)], out_sem.at[2 * i + 1]
-            ),
-        )
-
-    def tile_step(i):
-        start_row = pl.multiple_of(i * TILE, TILE)
-        own = pl.ds(start_row, TILE)
-        window = pl.ds(start_row, span)
-
-        slots = me * rows + start_row + lax.broadcasted_iota(jnp.int32, (1, TILE), 1)
+        copies = []
+        for pair in range(pairs):
+            lanes = pl.ds(pair * width, width)
+            for which, (source, target) in enumerate(((att, att_hbm), (gq, gq_hbm))):
+                copies.append(
+                    pltpu.make_async_copy(
+                        source.at[pair, tile_rows(i)],
+                        target.at[0, tile_rows(i), lanes],
+                        out_sem.at[i, pair, which],
+                    )
+                )
+        return copies
+
+    def tile_rows(i):
+        return pl.ds(pl.multiple_of(i * TILE, TILE), TILE)
+
+    def place(unit):
+        unit = jnp.clip(unit, 0, units - 1)
+        i = lax.rem(lax.div(unit, pairs) + tiles - 1, tiles)
+        return i, lax.rem(unit, pairs)
+
+    def slots_of(i):
+        return me * rows + i * TILE + lax.broadcasted_iota(jnp.int32, (1, TILE), 1)
+
+    def set_bias(i):
+        slots = slots_of(i)
         first = jnp.zeros((1, TILE), jnp.int32)
-        end = jnp.int32(0)
-        for r in range(responses):
-            end = end + lens_ref[0, r]
+        for end in ends:
             first = jnp.where(slots >= end, end, first)
-        live = jnp.where(slots < end, F32(1), F32(0))
-        live2 = jnp.concatenate([live] * PAIR, axis=1)
-        key_slots = (me - 1) * rows + start_row + lax.broadcasted_iota(jnp.int32, (span, TILE), 0)
+        key_slots = (me - 1) * rows + i * TILE + lax.broadcasted_iota(jnp.int32, (span, TILE), 0)
         seen = (key_slots >= first) & (key_slots <= slots)
-        one_bias = jnp.where(seen, F32(0), F32(HIDDEN))
+        bias[...] = jnp.where(seen, F32(0), F32(HIDDEN))
+
+    def heads_of(ref, pair, i):
+        return [ref[pair, tile_rows(i), k * dim : (k + 1) * dim] for k in range(PAIR)]
+
+    def put_heads(ref, pair, i, value_t):
         for k in range(PAIR):
-            bias[:, pl.ds(k * TILE, TILE)] = one_bias
-
-        k_w = win[window, :dim]
-        v_w = win[window, dim:]
-        k_p = pfx[:, :dim]
-        v_p = pfx[:, dim:]
-        kt_w = win_kt[:, window]
-        vt_w = win_vt[:, window]
-
-        q_parts, g_parts = [], []
-        wp_parts, ww_parts, sp_parts, sw_parts = [], [], [], []
-        for pair in range(heads // PAIR):
-            cols = [pl.ds((pair * PAIR + k) * dim, dim) for k in range(PAIR)]
-            q2 = jnp.concatenate([q_ref[own, c] for c in cols], axis=0)
-            up_t = jnp.concatenate([up_ref[own, c].T for c in cols], axis=1)
-            s_p = mm_nt(k_p, q2)
-            s_w = mm_nt(k_w, q2) + bias[...]
-            top = jnp.maximum(
-                jnp.max(s_p, axis=0, keepdims=True), jnp.max(s_w, axis=0, keepdims=True)
-            )
-            step = scale * math.log2(math.e)
-            w_p = jnp.exp2((s_p - top) * step).astype(BF16)
-            w_w = jnp.exp2((s_w - top) * step).astype(BF16)
-            mixed = mm(pfx_vt[...], w_p) + mm(vt_w, w_w)
-            inverse = live2 / mixed[dim : dim + 1]
-            att_t = (mixed[:dim] * inverse).astype(BF16)
-            g_t = (up_t.astype(F32) * inverse).astype(BF16)
-            delta = jnp.sum(g_t.astype(F32) * att_t.astype(F32), axis=0, keepdims=True)
-            d_p = (w_p.astype(F32) * (mm(v_p, g_t) - delta)).astype(BF16)
-            d_w = (w_w.astype(F32) * (mm(v_w, g_t) - delta)).astype(BF16)
-            gq_t = ((mm(pfx_kt[...], d_p) + mm(kt_w, d_w)) * (factor2 * scale)).astype(BF16)
-            for k, c in enumerate(cols):
-                att[own, c] = att_t[:, k * TILE : (k + 1) * TILE].T
-                gq[own, c] = gq_t[:, k * TILE : (k + 1) * TILE].T
-            q_parts.append(q2)
-            g_parts.append(g_t)
-            wp_parts.append(w_p)
-            ww_parts.append(w_w)
-            sp_parts.append(d_p)
-            sw_parts.append(d_w)
-        q_all = jnp.concatenate(q_parts, axis=0)
-        g_all = jnp.concatenate(g_parts, axis=1)
-        acc_p[:, :dim] += mm(jnp.concatenate(sp_parts, axis=1), q_all)
-        acc[window, :dim] += mm(jnp.concatenate(sw_parts, axis=1), q_all)
-        acc_p[:, dim:] += mm_nt(jnp.concatenate(wp_parts, axis=1), g_all)
-        acc[window, dim:] += mm_nt(jnp.concatenate(ww_parts, axis=1), g_all)
+            ref[pair, tile_rows(i), k * dim : (k + 1) * dim] = value_t[
+                :, k * TILE : (k + 1) * TILE
+            ].T
+
+    def pipeline_step(u):
+        a_tile, a_pair = place(u)
+        b_tile, b_pair = place(u - 1)
+        c_tile, _ = place(u - 2)
+        d_tile, d_pair = place(u - 3)
+        two = lambda v: lax.rem(v + 4, 2)
+        four = lambda v: lax.rem(v + 4, 4)
+        a_s, b_s = two(u), two(u - 1)
+        b_w, c_w, d_w = four(u - 1), four(u - 2), four(u - 3)
+        c_d, d_d = two(u - 2), two(u - 3)
+        low_rows, top_rows = pl.ds(prefix, span), pl.ds(0, prefix)
+
+        def window(i, lo=0, size=span):
+            return pl.ds(pl.multiple_of(i * TILE + lo, TILE), size)
+
+        q_a = jnp.concatenate(heads_of(q_ref, a_pair, a_tile), axis=0)
+        b_top = jnp.max(top_ref[b_s], axis=0, keepdims=True)
+        g_c = g_ref[c_w]
+        delta_c = delta_ref[two(u - 2), 0:1]
+        q_d = jnp.concatenate(heads_of(q_ref, d_pair, d_tile), axis=0)
+        g_d = g_ref[d_w]
+
+        tops = []
+        chunks = [(True, lo, min(TILE, prefix - lo)) for lo in range(0, prefix, TILE)]
+        chunks += [(False, lo, TILE) for lo in range(0, span, TILE)]
+
+        def piece(in_prefix, lo, size, i):
+            if in_prefix:
+                return pfx[pl.ds(lo, size)]
+            return win[window(i, lo, size)]
+
+        def chunk(in_prefix, lo, size):
+            at = pl.ds(lo if in_prefix else prefix + lo, size)
+            score = mm_nt(piece(in_prefix, lo, size, a_tile)[:, :dim], q_a)
+            if not in_prefix:
+                score = score + jnp.concatenate([bias[pl.ds(lo, size)]] * PAIR, axis=1)
+            s_ref[a_s, at] = score
+            tops.append(jnp.max(score.reshape(-1, 8, width), axis=0))
+            w_ref[b_w, at] = jnp.exp2((s_ref[b_s, at] - b_top) * step_scale).astype(BF16)
+            dp = mm(piece(in_prefix, lo, size, c_tile)[:, dim:], g_c) - delta_c
+            d_ref[c_d, at] = (w_ref[c_w, at].astype(F32) * dp).astype(BF16)
+
+        half = len(chunks) // 2
+        acc_p[:, :dim] += mm(d_ref[d_d, top_rows], q_d)
+        acc_p[:, dim:] += mm_nt(w_ref[d_w, top_rows], g_d)
+        for each in chunks[:half]:
+            chunk(*each)
+        acc[window(d_tile), :dim] += mm(d_ref[d_d, low_rows], q_d)
+        for each in chunks[half:]:
+            chunk(*each)
+        top_ref[a_s] = functools.reduce(jnp.maximum, tops)
+        mixed = mm(pfx_vt[...], w_ref[b_w, top_rows])
+        mixed = mixed + mm(win_vt[:, window(b_tile)], w_ref[b_w, low_rows])
+        acc[window(d_tile), dim:] += mm_nt(w_ref[d_w, low_rows], g_d)
+        gq_t = mm(pfx_kt[...], d_ref[d_d, top_rows])
+        gq_t = gq_t + mm(win_kt[:, window(d_tile)], d_ref[d_d, low_rows])
+        put_heads(gq, d_pair, d_tile, (gq_t * (factor2 * scale)).astype(BF16))
+
+        counted = jnp.where((slots_of(b_tile) < ends[-1]) & (u >= 1), F32(1), F32(0))
+        inverse = jnp.concatenate([counted] * PAIR, axis=1) / mixed[dim : dim + 1]
+        att_t = (mixed[:dim] * inverse).astype(BF16)
+        up_t = jnp.concatenate([v.T for v in heads_of(up_ref, b_pair, b_tile)], axis=1)
+        g_t = (up_t.astype(F32) * inverse).astype(BF16)
+        g_ref[b_w] = g_t
+        delta_ref[b_s, 0:1] = jnp.sum(g_t.astype(F32) * att_t.astype(F32), axis=0, keepdims=True)
+        put_heads(att, b_pair, b_tile, att_t)
 
     def give_back(j):
         ret_out[part(j)] = acc[part(j)].astype(BF16)
@@ -307,10 +370,12 @@
         def _():
             ret_copy(j).start()
 
-    def round_step(s, carry):
-        i = lax.rem(s + tiles - 1, tiles)
-
-        @pl.when(s == 1)
+    def loop_step(u, carry):
+        @pl.when((lax.rem(u, pairs) == 0) & (u < units))
+        def _():
+            set_bias(place(u)[0])
+
+        @pl.when(u == pairs)
         def _():
             @pl.when(has_prev)
             def _():
@@ -320,19 +385,22 @@
             for j in order[1:]:
                 turn(j)
 
-        tile_step(i)
-        for copy in out_copies(i):
-            copy.start()
-        for k in range(1, tiles - 1):
-
-            @pl.when(s == k)
+        for k in range(tiles - 1):
+
+            @pl.when(u == (k + 1) * pairs + 3)
             def _():
-                give_back(k - 1)
-
+                for copy in out_copies(order[k]):
+                    copy.start()
+                if k >= 1:
+                    give_back(k - 1)
+
+        pipeline_step(u)
         return carry
 
-    lax.fori_loop(0, tiles, round_step, 0)
-
+    lax.fori_loop(0, units + 3, loop_step, 0)
+
+    for copy in out_copies(order[-1]):
+        copy.start()
     gp_out[...] = acc_p[...].astype(BF16)
     for d, peer in enumerate(seq_peers):
         gp_copy(d, me, peer).start()
@@ -354,7 +422,7 @@
             ).wait_recv()
 
         gkv[part(j)] = (acc[part(tiles + j)] + ret_in[part(j)].astype(F32)) * final
-    gkv_copy = pltpu.make_async_copy(gkv, gkv_hbm.at[0], out_sem.at[2 * tiles])
+    gkv_copy = pltpu.make_async_copy(gkv, gkv_hbm.at[0], last_sem.at[0])
     gkv_copy.start()
 
     sums = acc_p[own_block]
@@ -362,7 +430,7 @@
         gp_copy(d, peer, me).wait_recv()
         sums = sums + gp_in[peer].astype(F32)
     gpf[...] = sums * final
-    gpf_copy = pltpu.make_async_copy(gpf, gpf_hbm.at[0], out_sem.at[2 * tiles + 1])
+    gpf_copy = pltpu.make_async_copy(gpf, gpf_hbm.at[0], last_sem.at[1])
     gpf_copy.start()
 
     for d, peer in enumerate(seq_peers):
@@ -386,6 +454,24 @@
             copy.wait()
     gkv_copy.wait()
     gpf_copy.wait()
+
+
+def hand_over(*refs):
+    half = (len(refs) - 1) // 2
+    sources, targets, sems = refs[:half], refs[half : 2 * half], refs[-1]
+    copies = []
+    for a, (source, target) in enumerate(zip(sources, targets)):
+        pieces = 4 if source.shape[1] % 64 == 0 else 1
+        step = source.shape[1] // pieces
+        for p in range(pieces):
+            rows = pl.ds(p * step, step)
+            copies.append(
+                pltpu.make_async_copy(source.at[0, rows], target.at[0, rows], sems.at[a, p])
+            )
+    for copy in copies:
+        copy.start()
+    for copy in copies:
+        copy.wait()
 
 
 def body(n_prompt, n_seq, queries, resp_kv, prefix_kv, lengths, upstream):
@@ -394,31 +480,41 @@
     block = prefix_kv.shape[1]
     prefix = block * n_seq
     tiles = rows // TILE
+    keys = prefix + rows + TILE
+    lanes = PAIR * dim
+    pairs = width // lanes
     dma = pltpu.SemaphoreType.DMA
     anywhere = pl.BlockSpec(memory_space=pl.ANY)
     vmem = pltpu.VMEM
-    return pl.pallas_call(
+    out_shape = (
+        jax.ShapeDtypeStruct(queries.shape, BF16),
+        jax.ShapeDtypeStruct(queries.shape, BF16),
+        jax.ShapeDtypeStruct(resp_kv.shape, F32),
+        jax.ShapeDtypeStruct(prefix_kv.shape, F32),
+    )
+    results = pl.pallas_call(
         functools.partial(kernel, n_prompt, n_seq),
-        out_shape=(
-            jax.ShapeDtypeStruct(queries.shape, BF16),
-            jax.ShapeDtypeStruct(queries.shape, BF16),
-            jax.ShapeDtypeStruct(resp_kv.shape, F32),
-            jax.ShapeDtypeStruct(prefix_kv.shape, F32),
-        ),
-        in_specs=[pl.BlockSpec(memory_space=pltpu.SMEM)] + [anywhere] * 4,
+        out_shape=out_shape,
+        in_specs=[pl.BlockSpec(memory_space=pltpu.SMEM)] + [pl.BlockSpec(memory_space=pltpu.HBM)] * 4,
         out_specs=(anywhere,) * 4,
         scratch_shapes=[
-            vmem((rows, width), BF16),
-            vmem((rows, width), BF16),
+            vmem((pairs, rows, lanes), BF16),
+            vmem((pairs, rows, lanes), BF16),
             vmem((2 * rows, 2 * dim), BF16),
             vmem((prefix, 2 * dim), BF16),
             vmem((dim, 2 * rows), BF16),
             vmem((dim + ONES, 2 * rows), BF16),
             vmem((dim, prefix), BF16),
             vmem((dim + ONES, prefix), BF16),
-            vmem((rows + TILE, PAIR * TILE), F32),
-            vmem((rows, width), BF16),
-            vmem((rows, width), BF16),
+            vmem((rows + TILE, TILE), F32),
+            vmem((2, keys, lanes), F32),
+            vmem((2, 8, lanes), F32),
+            vmem((4, keys, lanes), BF16),
+            vmem((4, dim, lanes), BF16),
+            vmem((2, 8, lanes), F32),
+            vmem((2, keys, lanes), BF16),
+            vmem((pairs, rows, lanes), BF16),
+            vmem((pairs, rows, lanes), BF16),
             vmem((2 * rows, 2 * dim), F32),
             vmem((prefix, 2 * dim), F32),
             vmem((rows, 2 * dim), BF16),
@@ -428,8 +524,9 @@
             vmem((rows, 2 * dim), F32),
             vmem((block, 2 * dim), F32),
             vmem((n_prompt, 8, 128), F32),
-            dma((4,)),
-            dma((2 * tiles + 2,)),
+            dma((2 + 2 * pairs,)),
+            dma((tiles, pairs, 2)),
+            dma((2,)),
             dma((n_seq,)),
             dma((n_seq,)),
             dma((tiles,)),
@@ -445,7 +542,15 @@
             collective_id=0, has_side_effects=True, vmem_limit_bytes=50 * 1024 * 1024
         ),
         name="attention_core",
-    )(lengths, queries, resp_kv, prefix_kv, upstream)
+    )(*[pltpu.with_memory_space_constraint(x, pltpu.HBM) for x in (lengths, queries, resp_kv, prefix_kv, upstream)])
+    return pl.pallas_call(
+        hand_over,
+        out_shape=out_shape,
+        in_specs=[pl.BlockSpec(memory_space=vmem)] * 4,
+        out_specs=(anywhere,) * 4,
+        scratch_shapes=[dma((4, 4))],
+        name="hand_over",
+    )(*results)
 
 
 def solution(mesh):

time: 42.7 us -> 50.3 us (1.18)
  Pallas kernels: 34.9 us -> 46.1 us
  local copies, waits for them, and re-layouts: 6.91 us -> 3.37 us
    pallas_call x1 -> x2, Pallas kernels: 34.9 us -> 46.1 us  [the longest x1 42.8 us: body(): pl.pallas_call(functools.partial(kernel, n_prompt, n_seq), out_shape=out_...]
    unnamed x12 -> x8, local copies, waits for them, and re-layouts: 6.91 us -> 3.37 us
where the time goes in v3:
time: 50.3 us; the launch traced here: 50.2 us
  Pallas kernels  46.1 us (92%)
  local copies, waits for them, and re-layouts  3.37 us (7%)
  between operations  0.65 us (1%)
    pallas_call x1, Pallas kernels, body(): pl.pallas_call(functools.partial(kernel, n_prompt, n_seq), out_shape=out_...  42.8 us
    unnamed x8, local copies, waits for them, and re-layouts  3.37 us
    pallas_call x1, Pallas kernels, body(): pl.pallas_call(hand_over, out_shape=out_shape, in_specs=[pl.BlockSpec(mem...  3.29 us

profile of v3, /device:TPU:1, one launch (start us, length us, event | category | flops | bytes accessed | tf_op | source)
XLA Modules:
  0.0 50.2 jit_solution(13231470914185943841)
XLA Ops:
  0.6 42.8 %attention_core.1 = (bf16[1,512,1024]{2,1,0:T(8,128)(2,1)S(1)}, bf16[1,512,1024]{2,1,0:T(8,128)(2,1)S(1)}, f32[1,512,256]{2,1,0:T(8,128)S(1)}, f32[1,48,256]{2,1,0:T(8,128)S(1)}) custom-call(s32[1,4]{1,0:T(1,128)} %lens_ref.1, bf16[1,512,1024]{2,1,0:T(8,128)(2,1)} %q_hbm.1, bf16[1,512,256]{2,1,0:T(8,128)(2,1)} %kv_hbm.1, bf16[1,48,256]{2,1,0:T(8,128)(2,1)} %pkv_hbm.1, ...), custom_call_target="tpu_custom_call" | custom-call | tf_op jit(solution)/shard_map/attention_core/pallas_call | solution.py:495
  43.5 0.0 copy-start
  43.5 1.0 %copy-done = bf16[1,512,1024]{2,1,0:T(8,128)(2,1)} copy-done((bf16[1,512,1024]{2,1,0:T(8,128)(2,1)}, bf16[1,512,1024]{2,1,0:T(8,128)(2,1)S(1)}, u32[]{:S(2)}) %copy-start) | copy-done | bytes 1048600
  44.5 0.0 copy-start.1
  44.5 1.0 %copy-done.1 = bf16[1,512,1024]{2,1,0:T(8,128)(2,1)} copy-done((bf16[1,512,1024]{2,1,0:T(8,128)(2,1)}, bf16[1,512,1024]{2,1,0:T(8,128)(2,1)S(1)}, u32[]{:S(2)}) %copy-start.1) | copy-done | bytes 1048600
  45.5 0.0 copy-start.2
  45.5 0.8 %copy-done.2 = f32[1,512,256]{2,1,0:T(8,128)} copy-done((f32[1,512,256]{2,1,0:T(8,128)}, f32[1,512,256]{2,1,0:T(8,128)S(1)}, u32[]{:S(2)}) %copy-start.2) | copy-done | bytes 524312
  46.3 0.0 copy-start.3
  46.3 0.6 %copy-done.3 = f32[1,48,256]{2,1,0:T(8,128)} copy-done((f32[1,48,256]{2,1,0:T(8,128)}, f32[1,48,256]{2,1,0:T(8,128)S(1)}, u32[]{:S(2)}) %copy-start.3) | copy-done | bytes 49176
  46.9 3.3 %hand_over.1 = (bf16[1,512,1024]{2,1,0:T(8,128)(2,1)}, bf16[1,512,1024]{2,1,0:T(8,128)(2,1)}, f32[1,512,256]{2,1,0:T(8,128)}, f32[1,48,256]{2,1,0:T(8,128)}) custom-call(bf16[1,512,1024]{2,1,0:T(8,128)(2,1)} %copy-done, bf16[1,512,1024]{2,1,0:T(8,128)(2,1)} %copy-done.1, f32[1,512,256]{2,1,0:T(8,128)} %copy-done.2, f32[1,48,256]{2,1,0:T(8,128)} %copy-done.3), custom_call_target="tpu_custom_call" | custom-call | tf_op jit(solution)/shard_map/hand_over/pallas_call | solution.py:546
Async XLA Ops:
  43.5 1.0 %copy-start = (bf16[1,512,1024]{2,1,0:T(8,128)(2,1)}, bf16[1,512,1024]{2,1,0:T(8,128)(2,1)S(1)}, u32[]{:S(2)}) copy-start(bf16[1,512,1024]{2,1,0:T(8,128)(2,1)S(1)} %get-tuple-element.8.refs_0_) | copy-start | bytes 3145732
  44.5 1.0 %copy-start.1 = (bf16[1,512,1024]{2,1,0:T(8,128)(2,1)}, bf16[1,512,1024]{2,1,0:T(8,128)(2,1)S(1)}, u32[]{:S(2)}) copy-start(bf16[1,512,1024]{2,1,0:T(8,128)(2,1)S(1)} %get-tuple-element.9.refs_1_) | copy-start | bytes 3145732
  45.5 0.8 %copy-start.2 = (f32[1,512,256]{2,1,0:T(8,128)}, f32[1,512,256]{2,1,0:T(8,128)S(1)}, u32[]{:S(2)}) copy-start(f32[1,512,256]{2,1,0:T(8,128)S(1)} %get-tuple-element.10.refs_2_) | copy-start | bytes 1572868
  46.3 0.6 %copy-start.3 = (f32[1,48,256]{2,1,0:T(8,128)}, f32[1,48,256]{2,1,0:T(8,128)S(1)}, u32[]{:S(2)}) copy-start(f32[1,48,256]{2,1,0:T(8,128)S(1)} %get-tuple-element.11.refs_3_) | copy-start | bytes 147460

commit v4 on v1

--- a/solution.py
+++ b/solution.py
@@ -45,6 +45,12 @@
     pfx_kt,
     pfx_vt,
     bias,
+    s_ref,
+    top_ref,
+    w_ref,
+    g_ref,
+    delta_ref,
+    d_ref,
     att,
     gq,
     acc,
@@ -74,6 +80,7 @@
     heads = q_ref.shape[1] // dim
     tiles = rows // TILE
     block = pkv_hbm.shape[1]
+    prefix = pfx.shape[0]
     span = rows + TILE
     responses = lens_ref.shape[1]
     scale = dim ** (-0.5)
@@ -99,11 +106,30 @@
     loads = [
         pltpu.make_async_copy(kv_hbm.at[0], win.at[pl.ds(rows, rows)], in_sem.at[0]),
         pltpu.make_async_copy(pkv_hbm.at[0], pfx.at[own_block], in_sem.at[1]),
-        pltpu.make_async_copy(q_hbm.at[0], q_ref, in_sem.at[2]),
-        pltpu.make_async_copy(up_hbm.at[0], up_ref, in_sem.at[3]),
     ]
     for load in loads:
         load.start()
+
+    def row_loads(i):
+        some = pl.ds(pl.multiple_of(i * TILE, TILE), TILE)
+        return (
+            pltpu.make_async_copy(q_hbm.at[0, some], q_ref.at[some], in_sem.at[2 + 2 * i]),
+            pltpu.make_async_copy(up_hbm.at[0, some], up_ref.at[some], in_sem.at[3 + 2 * i]),
+        )
+
+    order = [tiles - 1] + list(range(tiles - 1))
+    for i in order:
+        for load in row_loads(i):
+            load.start()
+
+    last = heads // PAIR - 1
+    late = pl.ds((last - 1) * PAIR * TILE, 2 * PAIR * TILE)
+    s_ref[last % 2] = jnp.zeros(s_ref.shape[1:], F32)
+    w_ref[:, late] = jnp.zeros((w_ref.shape[0], 2 * PAIR * TILE), BF16)
+    for pair in (last - 1, last):
+        top_ref[pair] = jnp.zeros(top_ref.shape[1:], F32)
+        g_ref[pair] = jnp.zeros(g_ref.shape[1:], BF16)
+        delta_ref[pair] = jnp.zeros(delta_ref.shape[1:], F32)
 
     total = lens_ref[0, 0]
     for r in range(1, responses):
@@ -168,7 +194,6 @@
             (my_p, target),
         )
 
-    order = [tiles - 1] + list(range(tiles - 1))
     for d, peer in enumerate(seq_peers):
         pf_copy(d, me, peer).start()
 
@@ -229,76 +254,129 @@
     def out_copies(i):
         return (
             pltpu.make_async_copy(
-                att.at[part(i)], att_hbm.at[0, part(i)], out_sem.at[2 * i]
+                att.at[tile_rows(i)], att_hbm.at[0, tile_rows(i)], out_sem.at[2 * i]
             ),
             pltpu.make_async_copy(
-                gq.at[part(i)], gq_hbm.at[0, part(i)], out_sem.at[2 * i + 1]
+                gq.at[tile_rows(i)], gq_hbm.at[0, tile_rows(i)], out_sem.at[2 * i + 1]
             ),
         )
 
-    def tile_step(i):
-        start_row = pl.multiple_of(i * TILE, TILE)
-        own = pl.ds(start_row, TILE)
-        window = pl.ds(start_row, span)
-
-        slots = me * rows + start_row + lax.broadcasted_iota(jnp.int32, (1, TILE), 1)
+    ends = []
+    for r in range(responses):
+        ends.append(lens_ref[0, r] + (ends[-1] if ends else 0))
+    pairs = heads // PAIR
+    width = PAIR * TILE
+    step_scale = scale * math.log2(math.e)
+    top_rows, low_rows = pl.ds(0, prefix), pl.ds(prefix, span)
+    chunks = [(True, lo, min(TILE, prefix - lo)) for lo in range(0, prefix, TILE)]
+    chunks += [(False, lo, TILE) for lo in range(0, span, TILE)]
+
+    def tile_rows(i, size=TILE, lo=0):
+        return pl.ds(pl.multiple_of(i * TILE + lo, TILE), size)
+
+    def slots_of(i):
+        return me * rows + i * TILE + lax.broadcasted_iota(jnp.int32, (1, TILE), 1)
+
+    def set_bias(i):
+        slots = slots_of(i)
         first = jnp.zeros((1, TILE), jnp.int32)
-        end = jnp.int32(0)
-        for r in range(responses):
-            end = end + lens_ref[0, r]
+        for end in ends:
             first = jnp.where(slots >= end, end, first)
-        live = jnp.where(slots < end, F32(1), F32(0))
-        live2 = jnp.concatenate([live] * PAIR, axis=1)
-        key_slots = (me - 1) * rows + start_row + lax.broadcasted_iota(jnp.int32, (span, TILE), 0)
+        key_slots = (me - 1) * rows + i * TILE + lax.broadcasted_iota(jnp.int32, (span, TILE), 0)
         seen = (key_slots >= first) & (key_slots <= slots)
-        one_bias = jnp.where(seen, F32(0), F32(HIDDEN))
-        for k in range(PAIR):
-            bias[:, pl.ds(k * TILE, TILE)] = one_bias
-
-        k_w = win[window, :dim]
-        v_w = win[window, dim:]
-        k_p = pfx[:, :dim]
-        v_p = pfx[:, dim:]
-        kt_w = win_kt[:, window]
-        vt_w = win_vt[:, window]
-
-        q_parts, g_parts = [], []
-        wp_parts, ww_parts, sp_parts, sw_parts = [], [], [], []
-        for pair in range(heads // PAIR):
-            cols = [pl.ds((pair * PAIR + k) * dim, dim) for k in range(PAIR)]
-            q2 = jnp.concatenate([q_ref[own, c] for c in cols], axis=0)
-            up_t = jnp.concatenate([up_ref[own, c].T for c in cols], axis=1)
-            s_p = mm_nt(k_p, q2)
-            s_w = mm_nt(k_w, q2) + bias[...]
-            top = jnp.maximum(
-                jnp.max(s_p, axis=0, keepdims=True), jnp.max(s_w, axis=0, keepdims=True)
+        bias[...] = jnp.where(seen, F32(0), F32(HIDDEN))
+
+    def cols_of(pair):
+        return [pl.ds((pair * PAIR + k) * dim, dim) for k in range(PAIR)]
+
+    def heads_of(ref, pair, i):
+        return [ref[tile_rows(i), c] for c in cols_of(pair)]
+
+    def put_heads(ref, pair, i, value_t):
+        for k, c in enumerate(cols_of(pair)):
+            ref[tile_rows(i), c] = value_t[:, k * TILE : (k + 1) * TILE].T
+
+    def piece(in_prefix, lo, size, i):
+        if in_prefix:
+            return pfx[pl.ds(lo, size)]
+        return win[tile_rows(i, size, lo)]
+
+    def place_of(in_prefix, lo, size):
+        return pl.ds(lo if in_prefix else prefix + lo, size)
+
+    def score_stage(pair, i):
+        q_a = jnp.concatenate(heads_of(q_ref, pair, i), axis=0)
+        tops = []
+
+        def chunk(in_prefix, lo, size):
+            score = mm_nt(piece(in_prefix, lo, size, i)[:, :dim], q_a)
+            if not in_prefix:
+                score = score + jnp.concatenate([bias[pl.ds(lo, size)]] * PAIR, axis=1)
+            s_ref[pair % 2, place_of(in_prefix, lo, size)] = score
+            tops.append(jnp.max(score.reshape(-1, 8, width), axis=0))
+
+        def end():
+            top_ref[pair] = functools.reduce(jnp.maximum, tops)
+
+        return chunk, end
+
+    def weight_stage(pair, i, counts):
+        lanes = pl.ds(pair * width, width)
+        top = jnp.max(top_ref[pair], axis=0, keepdims=True)
+
+        def chunk(in_prefix, lo, size):
+            at = place_of(in_prefix, lo, size)
+            w_ref[at, lanes] = jnp.exp2((s_ref[pair % 2, at] - top) * step_scale).astype(BF16)
+
+        def end():
+            mixed = mm(pfx_vt[...], w_ref[top_rows, lanes])
+            mixed = mixed + mm(win_vt[:, tile_rows(i, span)], w_ref[low_rows, lanes])
+            live = jnp.where((slots_of(i) < ends[-1]) & counts, F32(1), F32(0))
+            inverse = jnp.concatenate([live] * PAIR, axis=1) / mixed[dim : dim + 1]
+            att_t = (mixed[:dim] * inverse).astype(BF16)
+            up_t = jnp.concatenate([v.T for v in heads_of(up_ref, pair, i)], axis=1)
+            g_t = (up_t.astype(F32) * inverse).astype(BF16)
+            g_ref[pair] = g_t
+            delta_ref[pair, 0:1] = jnp.sum(
+                g_t.astype(F32) * att_t.astype(F32), axis=0, keepdims=True
             )
-            step = scale * math.log2(math.e)
-            w_p = jnp.exp2((s_p - top) * step).astype(BF16)
-            w_w = jnp.exp2((s_w - top) * step).astype(BF16)
-            mixed = mm(pfx_vt[...], w_p) + mm(vt_w, w_w)
-            inverse = live2 / mixed[dim : dim + 1]
-            att_t = (mixed[:dim] * inverse).astype(BF16)
-            g_t = (up_t.astype(F32) * inverse).astype(BF16)
-            delta = jnp.sum(g_t.astype(F32) * att_t.astype(F32), axis=0, keepdims=True)
-            d_p = (w_p.astype(F32) * (mm(v_p, g_t) - delta)).astype(BF16)
-            d_w = (w_w.astype(F32) * (mm(v_w, g_t) - delta)).astype(BF16)
-            gq_t = ((mm(pfx_kt[...], d_p) + mm(kt_w, d_w)) * (factor2 * scale)).astype(BF16)
-            for k, c in enumerate(cols):
-                att[own, c] = att_t[:, k * TILE : (k + 1) * TILE].T
-                gq[own, c] = gq_t[:, k * TILE : (k + 1) * TILE].T
-            q_parts.append(q2)
-            g_parts.append(g_t)
-            wp_parts.append(w_p)
-            ww_parts.append(w_w)
-            sp_parts.append(d_p)
-            sw_parts.append(d_w)
-        q_all = jnp.concatenate(q_parts, axis=0)
-        g_all = jnp.concatenate(g_parts, axis=1)
-        acc_p[:, :dim] += mm(jnp.concatenate(sp_parts, axis=1), q_all)
-        acc[window, :dim] += mm(jnp.concatenate(sw_parts, axis=1), q_all)
-        acc_p[:, dim:] += mm_nt(jnp.concatenate(wp_parts, axis=1), g_all)
-        acc[window, dim:] += mm_nt(jnp.concatenate(ww_parts, axis=1), g_all)
+            put_heads(att, pair, i, att_t)
+
+        return chunk, end
+
+    def grad_stage(pair, i):
+        lanes = pl.ds(pair * width, width)
+        g_c = g_ref[pair]
+        delta_c = delta_ref[pair, 0:1]
+
+        def chunk(in_prefix, lo, size):
+            at = place_of(in_prefix, lo, size)
+            dp = mm(piece(in_prefix, lo, size, i)[:, dim:], g_c) - delta_c
+            d_ref[at, lanes] = (w_ref[at, lanes].astype(F32) * dp).astype(BF16)
+
+        def end():
+            gq_t = mm(pfx_kt[...], d_ref[top_rows, lanes])
+            gq_t = gq_t + mm(win_kt[:, tile_rows(i, span)], d_ref[low_rows, lanes])
+            put_heads(gq, pair, i, (gq_t * (factor2 * scale)).astype(BF16))
+            if pair % 2 == 1:
+                both = pl.ds((pair - 1) * width, 2 * width)
+                q_all = jnp.concatenate(
+                    heads_of(q_ref, pair - 1, i) + heads_of(q_ref, pair, i), axis=0
+                )
+                g_all = jnp.concatenate([g_ref[pair - 1], g_ref[pair]], axis=1)
+                acc_p[:, :dim] += mm(d_ref[top_rows, both], q_all)
+                acc[tile_rows(i, span), :dim] += mm(d_ref[low_rows, both], q_all)
+                acc_p[:, dim:] += mm_nt(w_ref[top_rows, both], g_all)
+                acc[tile_rows(i, span), dim:] += mm_nt(w_ref[low_rows, both], g_all)
+
+        return chunk, end
+
+    def run(stages):
+        for each in chunks:
+            for chunk, _ in stages:
+                chunk(*each)
+        for _, end in stages:
+            end()
 
     def give_back(j):
         ret_out[part(j)] = acc[part(j)].astype(BF16)
@@ -307,10 +385,13 @@
         def _():
             ret_copy(j).start()
 
-    def round_step(s, carry):
-        i = lax.rem(s + tiles - 1, tiles)
-
-        @pl.when(s == 1)
+    def tile_at(k):
+        return lax.rem(k + tiles - 1, tiles)
+
+    def round_step(k, carry):
+        i, before = tile_at(k), tile_at(jnp.maximum(k - 1, 0))
+
+        @pl.when(k == 1)
         def _():
             @pl.when(has_prev)
             def _():
@@ -320,19 +401,44 @@
             for j in order[1:]:
                 turn(j)
 
-        tile_step(i)
-        for copy in out_copies(i):
-            copy.start()
-        for k in range(1, tiles - 1):
-
-            @pl.when(s == k)
+        for load in row_loads(i):
+            load.wait()
+
+        @pl.when(k >= 2)
+        def _():
+            for copy in out_copies(tile_at(k - 2)):
+                copy.start()
+
+        for r in range(3, tiles):
+
+            @pl.when(k == r)
             def _():
-                give_back(k - 1)
-
+                give_back(r - 3)
+
+        set_bias(i)
+        for pair in range(pairs):
+            stages = [score_stage(pair, i)]
+            if pair >= 1:
+                stages.append(weight_stage(pair - 1, i, True))
+            else:
+                stages.append(weight_stage(pairs - 1, before, k >= 1))
+            if pair >= 2:
+                stages.append(grad_stage(pair - 2, i))
+            else:
+                stages.append(grad_stage(pairs - 2 + pair, before))
+            run(stages)
         return carry
 
     lax.fori_loop(0, tiles, round_step, 0)
 
+    for copy in out_copies(order[-2]):
+        copy.start()
+    for j in range(max(tiles - 3, 0), tiles - 2):
+        give_back(j)
+    run([weight_stage(pairs - 1, order[-1], True), grad_stage(pairs - 2, order[-1])])
+    run([grad_stage(pairs - 1, order[-1])])
+    for copy in out_copies(order[-1]):
+        copy.start()
     gp_out[...] = acc_p[...].astype(BF16)
     for d, peer in enumerate(seq_peers):
         gp_copy(d, me, peer).start()
@@ -394,17 +500,23 @@
     block = prefix_kv.shape[1]
     prefix = block * n_seq
     tiles = rows // TILE
+    pairs = width // (PAIR * dim)
     dma = pltpu.SemaphoreType.DMA
     anywhere = pl.BlockSpec(memory_space=pl.ANY)
     vmem = pltpu.VMEM
+    out_shape = (
+        jax.ShapeDtypeStruct(queries.shape, BF16),
+        jax.ShapeDtypeStruct(queries.shape, BF16),
+        jax.ShapeDtypeStruct(resp_kv.shape, F32),
+        jax.ShapeDtypeStruct(prefix_kv.shape, F32),
+    )
+    placed = [
+        pltpu.with_memory_space_constraint(x, pltpu.HBM)
+        for x in (lengths, queries, resp_kv, prefix_kv, upstream)
+    ]
     return pl.pallas_call(
         functools.partial(kernel, n_prompt, n_seq),
-        out_shape=(
-            jax.ShapeDtypeStruct(queries.shape, BF16),
-            jax.ShapeDtypeStruct(queries.shape, BF16),
-            jax.ShapeDtypeStruct(resp_kv.shape, F32),
-            jax.ShapeDtypeStruct(prefix_kv.shape, F32),
-        ),
+        out_shape=out_shape,
         in_specs=[pl.BlockSpec(memory_space=pltpu.SMEM)] + [anywhere] * 4,
         out_specs=(anywhere,) * 4,
         scratch_shapes=[
@@ -416,7 +528,13 @@
             vmem((dim + ONES, 2 * rows), BF16),
             vmem((dim, prefix), BF16),
             vmem((dim + ONES, prefix), BF16),
-            vmem((rows + TILE, PAIR * TILE), F32),
+            vmem((rows + TILE, TILE), F32),
+            vmem((2, prefix + rows + TILE, PAIR * TILE), F32),
+            vmem((pairs, 8, PAIR * TILE), F32),
+            vmem((prefix + rows + TILE, width), BF16),
+            vmem((pairs, dim, PAIR * TILE), BF16),
+            vmem((pairs, 8, PAIR * TILE), F32),
+            vmem((prefix + rows + TILE, width), BF16),
             vmem((rows, width), BF16),
             vmem((rows, width), BF16),
             vmem((2 * rows, 2 * dim), F32),
@@ -428,7 +546,7 @@
             vmem((rows, 2 * dim), F32),
             vmem((block, 2 * dim), F32),
             vmem((n_prompt, 8, 128), F32),
-            dma((4,)),
+            dma((2 + 2 * tiles,)),
             dma((2 * tiles + 2,)),
             dma((n_seq,)),
             dma((n_seq,)),
@@ -445,7 +563,7 @@
             collective_id=0, has_side_effects=True, vmem_limit_bytes=50 * 1024 * 1024
         ),
         name="attention_core",
-    )(lengths, queries, resp_kv, prefix_kv, upstream)
+    )(*placed)
 
 
 def solution(mesh):

time: 42.7 us -> 35.7 us (0.84)
  local copies, waits for them, and re-layouts: 6.91 us -> 3.35 us
  Pallas kernels: 34.9 us -> 31.6 us
    unnamed x12 -> x4, local copies, waits for them, and re-layouts: 6.91 us -> 3.35 us
    pallas_call x1, Pallas kernels: 34.9 us -> 31.6 us  [body(): pl.pallas_call(functools.partial(kernel, n_prompt, n_seq), out_shape=out_...]
where the time goes in v4:
time: 35.7 us; the launch traced here: 35.5 us
  Pallas kernels  31.6 us (89%)
  local copies, waits for them, and re-layouts  3.35 us (9%)
  between operations  0.64 us (2%)
    pallas_call x1, Pallas kernels, body(): pl.pallas_call(functools.partial(kernel, n_prompt, n_seq), out_shape=out_...  31.6 us
    unnamed x4, local copies, waits for them, and re-layouts  3.35 us

profile of v4, /device:TPU:1, one launch (start us, length us, event | category | flops | bytes accessed | tf_op | source)
XLA Modules:
  0.0 35.5 jit_solution(4285617962746101781)
XLA Ops:
  0.6 31.6 %attention_core.1 = (bf16[1,512,1024]{2,1,0:T(8,128)(2,1)S(1)}, bf16[1,512,1024]{2,1,0:T(8,128)(2,1)S(1)}, f32[1,512,256]{2,1,0:T(8,128)S(1)}, f32[1,48,256]{2,1,0:T(8,128)S(1)}) custom-call(s32[1,4]{1,0:T(1,128)} %lens_ref.1, bf16[1,512,1024]{2,1,0:T(8,128)(2,1)} %q_hbm.1, bf16[1,512,256]{2,1,0:T(8,128)(2,1)} %kv_hbm.1, bf16[1,48,256]{2,1,0:T(8,128)(2,1)} %pkv_hbm.1, ...), custom_call_target="tpu_custom_call" | custom-call | tf_op jit(solution)/shard_map/attention_core/pallas_call | solution.py:517
  32.2 1.0 %copy.13 = bf16[1,512,1024]{2,1,0:T(8,128)(2,1)} copy(bf16[1,512,1024]{2,1,0:T(8,128)(2,1)S(1)} %get-tuple-element.8) | data formatting | bytes 2097152
  33.2 1.0 %copy.14 = bf16[1,512,1024]{2,1,0:T(8,128)(2,1)} copy(bf16[1,512,1024]{2,1,0:T(8,128)(2,1)S(1)} %get-tuple-element.9) | data formatting | bytes 2097152
  34.1 0.8 %copy.15 = f32[1,512,256]{2,1,0:T(8,128)} copy(f32[1,512,256]{2,1,0:T(8,128)S(1)} %get-tuple-element.10) | data formatting | bytes 1048576
  34.9 0.6 %copy.16 = f32[1,48,256]{2,1,0:T(8,128)} copy(f32[1,48,256]{2,1,0:T(8,128)S(1)} %get-tuple-element.11) | data formatting | bytes 98304

commit v5 on v3

--- a/solution.py
+++ b/solution.py
@@ -13,6 +13,7 @@
 TILE = 128
 HIDDEN = -1e30
 PAIR = 2
+CHUNK = 128
 ONES = 16
 
 
@@ -22,6 +23,13 @@
 
 def mm_nt(a, b):
     return lax.dot_general(a, b, (((1,), (1,)), ((), ())), preferred_element_type=F32)
+
+
+def clear(ref, size):
+    @pl.loop(0, size // 64)
+    def _(j):
+        at = pl.ds(pl.multiple_of(j * 64, 64), 64)
+        ref[at] = jnp.zeros((64,) + ref.shape[1:], ref.dtype)
 
 
 def kernel(
@@ -62,6 +70,7 @@
     gkv,
     gpf,
     lens_all,
+    own_sem,
     in_sem,
     out_sem,
     last_sem,
@@ -104,27 +113,32 @@
 
     own_block = pl.ds(pl.multiple_of(me * block, 16), block)
     loads = [
-        pltpu.make_async_copy(kv_hbm.at[0], win.at[pl.ds(rows, rows)], in_sem.at[0]),
-        pltpu.make_async_copy(pkv_hbm.at[0], pfx.at[own_block], in_sem.at[1]),
+        pltpu.make_async_copy(kv_hbm.at[0], win.at[pl.ds(rows, rows)], own_sem.at[0]),
+        pltpu.make_async_copy(pkv_hbm.at[0], pfx.at[own_block], own_sem.at[1]),
     ]
-    for pair in range(pairs):
-        lanes = pl.ds(pair * width, width)
-        for k, (source, target) in enumerate(((q_hbm, q_ref), (up_hbm, up_ref))):
-            loads.append(
-                pltpu.make_async_copy(
-                    source.at[0, :, lanes], target.at[pair], in_sem.at[2 + 2 * pair + k]
+
+    def row_loads(some, group):
+        copies = []
+        for pair in range(pairs):
+            lanes = pl.ds(pair * width, width)
+            for k, (source, target) in enumerate(((q_hbm, q_ref), (up_hbm, up_ref))):
+                copies.append(
+                    pltpu.make_async_copy(
+                        source.at[0, some, lanes], target.at[pair, some], in_sem.at[group, pair, k]
+                    )
                 )
-            )
-    for load in loads:
+        return copies
+
+    order = [tiles - 1] + list(range(tiles - 1))
+    early_rows = row_loads(pl.ds((tiles - 1) * TILE, TILE), 0)
+    other_rows = row_loads(pl.ds(0, (tiles - 1) * TILE), 1)
+    for load in loads + early_rows + other_rows:
         load.start()
 
-    s_ref[1] = jnp.zeros(s_ref.shape[1:], F32)
-    top_ref[1] = jnp.zeros(top_ref.shape[1:], F32)
-    for slot in (1, 2):
-        w_ref[slot] = jnp.zeros(w_ref.shape[1:], BF16)
-        g_ref[slot] = jnp.zeros(g_ref.shape[1:], BF16)
-    delta_ref[0] = jnp.zeros(delta_ref.shape[1:], F32)
-    d_ref[1] = jnp.zeros(d_ref.shape[1:], BF16)
+    for ref in (top_ref, g_ref, delta_ref):
+        ref[...] = jnp.zeros_like(ref)
+    clear(s_ref, s_ref.shape[0])
+    clear(w_ref, w_ref.shape[0])
 
     total = lens_ref[0, 0]
     for r in range(1, responses):
@@ -144,7 +158,7 @@
         )
 
     def part(j):
-        return pl.ds(j * TILE, TILE)
+        return pl.ds(pl.multiple_of(j * TILE, TILE), TILE)
 
     def prev_copy(j):
         return remote(
@@ -189,7 +203,6 @@
             (my_p, target),
         )
 
-    order = [tiles - 1] + list(range(tiles - 1))
     for d, peer in enumerate(seq_peers):
         pf_copy(d, me, peer).start()
 
@@ -207,14 +220,14 @@
 
     @pl.when(jnp.logical_not(has_prev))
     def _():
-        win[pl.ds(0, rows)] = jnp.zeros((rows, 2 * dim), BF16)
+        clear(win, rows)
 
     @pl.when(jnp.logical_not(has_next))
     def _():
-        ret_in[...] = jnp.zeros((rows, 2 * dim), BF16)
-
-    acc[...] = jnp.zeros_like(acc)
-    acc_p[...] = jnp.zeros_like(acc_p)
+        clear(ret_in, rows)
+
+    clear(acc, 2 * rows)
+    clear(acc_p, prefix)
     win_vt[pl.ds(dim, ONES)] = jnp.ones((ONES, 2 * rows), BF16)
     pfx_vt[pl.ds(dim, ONES)] = jnp.ones((ONES, pfx.shape[0]), BF16)
 
@@ -225,9 +238,8 @@
         win_vt[pl.ds(0, dim), part(j)] = values.T
 
     loads[0].wait()
-    for j in range(tiles, 2 * tiles):
-        turn(j)
-    for load in loads[1:]:
+    pl.loop(tiles, 2 * tiles)(turn)
+    for load in loads[1:] + early_rows:
         load.wait()
     for d, peer in enumerate(seq_peers):
         pf_copy(d, peer, me).wait_recv()
@@ -296,72 +308,60 @@
                 :, k * TILE : (k + 1) * TILE
             ].T
 
+    def window(i, lo=0, size=span):
+        return pl.ds(pl.multiple_of(i * TILE + lo, TILE), size)
+
+    low_rows, top_rows = pl.ds(prefix, span), pl.ds(0, prefix)
+    chunks = [(True, lo, min(CHUNK, prefix - lo)) for lo in range(0, prefix, CHUNK)]
+    chunks += [(False, lo, min(CHUNK, span - lo)) for lo in range(0, span, CHUNK)]
+
     def pipeline_step(u):
         a_tile, a_pair = place(u)
         b_tile, b_pair = place(u - 1)
-        c_tile, _ = place(u - 2)
-        d_tile, d_pair = place(u - 3)
-        two = lambda v: lax.rem(v + 4, 2)
-        four = lambda v: lax.rem(v + 4, 4)
-        a_s, b_s = two(u), two(u - 1)
-        b_w, c_w, d_w = four(u - 1), four(u - 2), four(u - 3)
-        c_d, d_d = two(u - 2), two(u - 3)
-        low_rows, top_rows = pl.ds(prefix, span), pl.ds(0, prefix)
-
-        def window(i, lo=0, size=span):
-            return pl.ds(pl.multiple_of(i * TILE + lo, TILE), size)
-
+        c_tile, c_pair = place(u - 2)
         q_a = jnp.concatenate(heads_of(q_ref, a_pair, a_tile), axis=0)
-        b_top = jnp.max(top_ref[b_s], axis=0, keepdims=True)
-        g_c = g_ref[c_w]
-        delta_c = delta_ref[two(u - 2), 0:1]
-        q_d = jnp.concatenate(heads_of(q_ref, d_pair, d_tile), axis=0)
-        g_d = g_ref[d_w]
+        q_c = jnp.concatenate(heads_of(q_ref, c_pair, c_tile), axis=0)
+        b_top = jnp.max(top_ref[...], axis=0, keepdims=True)
+        g_c = g_ref[...]
+        delta_c = delta_ref[0:1]
+
+        acc_p[:, dim:] += mm_nt(w_ref[top_rows], g_c)
+        acc[window(c_tile), dim:] += mm_nt(w_ref[low_rows], g_c)
 
         tops = []
-        chunks = [(True, lo, min(TILE, prefix - lo)) for lo in range(0, prefix, TILE)]
-        chunks += [(False, lo, TILE) for lo in range(0, span, TILE)]
-
-        def piece(in_prefix, lo, size, i):
+        for in_prefix, lo, size in chunks:
+            at = pl.ds(lo if in_prefix else prefix + lo, size)
             if in_prefix:
-                return pfx[pl.ds(lo, size)]
-            return win[window(i, lo, size)]
-
-        def chunk(in_prefix, lo, size):
-            at = pl.ds(lo if in_prefix else prefix + lo, size)
-            score = mm_nt(piece(in_prefix, lo, size, a_tile)[:, :dim], q_a)
+                keys, values = pfx[pl.ds(lo, size), :dim], pfx[pl.ds(lo, size), dim:]
+            else:
+                keys = win[window(a_tile, lo, size), :dim]
+                values = win[window(c_tile, lo, size), dim:]
+            dp = mm(values, g_c) - delta_c
+            d_ref[at] = (w_ref[at].astype(F32) * dp).astype(BF16)
+            w_ref[at] = jnp.exp2((s_ref[at] - b_top) * step_scale).astype(BF16)
+            score = mm_nt(keys, q_a)
             if not in_prefix:
                 score = score + jnp.concatenate([bias[pl.ds(lo, size)]] * PAIR, axis=1)
-            s_ref[a_s, at] = score
+            s_ref[at] = score
             tops.append(jnp.max(score.reshape(-1, 8, width), axis=0))
-            w_ref[b_w, at] = jnp.exp2((s_ref[b_s, at] - b_top) * step_scale).astype(BF16)
-            dp = mm(piece(in_prefix, lo, size, c_tile)[:, dim:], g_c) - delta_c
-            d_ref[c_d, at] = (w_ref[c_w, at].astype(F32) * dp).astype(BF16)
-
-        half = len(chunks) // 2
-        acc_p[:, :dim] += mm(d_ref[d_d, top_rows], q_d)
-        acc_p[:, dim:] += mm_nt(w_ref[d_w, top_rows], g_d)
-        for each in chunks[:half]:
-            chunk(*each)
-        acc[window(d_tile), :dim] += mm(d_ref[d_d, low_rows], q_d)
-        for each in chunks[half:]:
-            chunk(*each)
-        top_ref[a_s] = functools.reduce(jnp.maximum, tops)
-        mixed = mm(pfx_vt[...], w_ref[b_w, top_rows])
-        mixed = mixed + mm(win_vt[:, window(b_tile)], w_ref[b_w, low_rows])
-        acc[window(d_tile), dim:] += mm_nt(w_ref[d_w, low_rows], g_d)
-        gq_t = mm(pfx_kt[...], d_ref[d_d, top_rows])
-        gq_t = gq_t + mm(win_kt[:, window(d_tile)], d_ref[d_d, low_rows])
-        put_heads(gq, d_pair, d_tile, (gq_t * (factor2 * scale)).astype(BF16))
+        top_ref[...] = functools.reduce(jnp.maximum, tops)
+
+        mixed = mm(pfx_vt[...], w_ref[top_rows])
+        mixed = mixed + mm(win_vt[:, window(b_tile)], w_ref[low_rows])
+        gq_t = mm(pfx_kt[...], d_ref[top_rows])
+        gq_t = gq_t + mm(win_kt[:, window(c_tile)], d_ref[low_rows])
+        acc_p[:, :dim] += mm(d_ref[top_rows], q_c)
+        acc[window(c_tile), :dim] += mm(d_ref[low_rows], q_c)
 
         counted = jnp.where((slots_of(b_tile) < ends[-1]) & (u >= 1), F32(1), F32(0))
         inverse = jnp.concatenate([counted] * PAIR, axis=1) / mixed[dim : dim + 1]
         att_t = (mixed[:dim] * inverse).astype(BF16)
         up_t = jnp.concatenate([v.T for v in heads_of(up_ref, b_pair, b_tile)], axis=1)
         g_t = (up_t.astype(F32) * inverse).astype(BF16)
-        g_ref[b_w] = g_t
-        delta_ref[b_s, 0:1] = jnp.sum(g_t.astype(F32) * att_t.astype(F32), axis=0, keepdims=True)
+        g_ref[...] = g_t
+        delta_ref[0:1] = jnp.sum(g_t.astype(F32) * att_t.astype(F32), axis=0, keepdims=True)
         put_heads(att, b_pair, b_tile, att_t)
+        put_heads(gq, c_pair, c_tile, (gq_t * (factor2 * scale)).astype(BF16))
 
     def give_back(j):
         ret_out[part(j)] = acc[part(j)].astype(BF16)
@@ -377,17 +377,19 @@
 
         @pl.when(u == pairs)
         def _():
+            for load in other_rows:
+                load.wait()
+
             @pl.when(has_prev)
             def _():
                 for j in order[1:]:
                     prev_copy(j).wait_recv()
 
-            for j in order[1:]:
-                turn(j)
+            pl.loop(0, tiles - 1)(turn)
 
         for k in range(tiles - 1):
 
-            @pl.when(u == (k + 1) * pairs + 3)
+            @pl.when(u == (k + 1) * pairs + 2)
             def _():
                 for copy in out_copies(order[k]):
                     copy.start()
@@ -397,7 +399,7 @@
         pipeline_step(u)
         return carry
 
-    lax.fori_loop(0, units + 3, loop_step, 0)
+    lax.fori_loop(0, units + 2, loop_step, 0)
 
     for copy in out_copies(order[-1]):
         copy.start()
@@ -408,8 +410,8 @@
         give_back(j)
 
     final = jnp.concatenate([factor * scale, factor], axis=1)
-    for j in range(tiles):
-
+    @pl.loop(0, tiles)
+    def _(j):
         @pl.when(has_next)
         def _():
             pltpu.make_async_remote_copy(
@@ -454,24 +456,6 @@
             copy.wait()
     gkv_copy.wait()
     gpf_copy.wait()
-
-
-def hand_over(*refs):
-    half = (len(refs) - 1) // 2
-    sources, targets, sems = refs[:half], refs[half : 2 * half], refs[-1]
-    copies = []
-    for a, (source, target) in enumerate(zip(sources, targets)):
-        pieces = 4 if source.shape[1] % 64 == 0 else 1
-        step = source.shape[1] // pieces
-        for p in range(pieces):
-            rows = pl.ds(p * step, step)
-            copies.append(
-                pltpu.make_async_copy(source.at[0, rows], target.at[0, rows], sems.at[a, p])
-            )
-    for copy in copies:
-        copy.start()
-    for copy in copies:
-        copy.wait()
 
 
 def body(n_prompt, n_seq, queries, resp_kv, prefix_kv, lengths, upstream):
@@ -492,7 +476,11 @@
         jax.ShapeDtypeStruct(resp_kv.shape, F32),
         jax.ShapeDtypeStruct(prefix_kv.shape, F32),
     )
-    results = pl.pallas_call(
+    placed = [
+        pltpu.with_memory_space_constraint(x, pltpu.HBM)
+        for x in (lengths, queries, resp_kv, prefix_kv, upstream)
+    ]
+    return pl.pallas_call(
         functools.partial(kernel, n_prompt, n_seq),
         out_shape=out_shape,
         in_specs=[pl.BlockSpec(memory_space=pltpu.SMEM)] + [pl.BlockSpec(memory_space=pltpu.HBM)] * 4,
@@ -507,12 +495,12 @@
             vmem((dim, prefix), BF16),
             vmem((dim + ONES, prefix), BF16),
             vmem((rows + TILE, TILE), F32),
-            vmem((2, keys, lanes), F32),
-            vmem((2, 8, lanes), F32),
-            vmem((4, keys, lanes), BF16),
-            vmem((4, dim, lanes), BF16),
-            vmem((2, 8, lanes), F32),
-            vmem((2, keys, lanes), BF16),
+            vmem((keys, lanes), F32),
+            vmem((8, lanes), F32),
+            vmem((keys, lanes), BF16),
+            vmem((dim, lanes), BF16),
+            vmem((8, lanes), F32),
+            vmem((keys, lanes), BF16),
             vmem((pairs, rows, lanes), BF16),
             vmem((pairs, rows, lanes), BF16),
             vmem((2 * rows, 2 * dim), F32),
@@ -524,7 +512,8 @@
             vmem((rows, 2 * dim), F32),
             vmem((block, 2 * dim), F32),
             vmem((n_prompt, 8, 128), F32),
-            dma((2 + 2 * pairs,)),
+            dma((2,)),
+            dma((2, pairs, 2)),
             dma((tiles, pairs, 2)),
             dma((2,)),
             dma((n_seq,)),
@@ -542,15 +531,7 @@
             collective_id=0, has_side_effects=True, vmem_limit_bytes=50 * 1024 * 1024
         ),
         name="attention_core",
-    )(*[pltpu.with_memory_space_constraint(x, pltpu.HBM) for x in (lengths, queries, resp_kv, prefix_kv, upstream)])
-    return pl.pallas_call(
-        hand_over,
-        out_shape=out_shape,
-        in_specs=[pl.BlockSpec(memory_space=vmem)] * 4,
-        out_specs=(anywhere,) * 4,
-        scratch_shapes=[dma((4, 4))],
-        name="hand_over",
-    )(*results)
+    )(*placed)
 
 
 def solution(mesh):

time: 50.3 us -> 35.2 us (0.70)
  Pallas kernels: 46.1 us -> 31 us
    pallas_call x1, Pallas kernels: 42.8 us -> 31 us  [body(): pl.pallas_call(functools.partial(kernel, n_prompt, n_seq), out_shape=out_...]
    pallas_call x1 -> x0, Pallas kernels: 3.29 us -> none  [body(): pl.pallas_call(hand_over, out_shape=out_shape, in_specs=[pl.BlockSpec(mem...]
    unnamed x8 -> x4, local copies, waits for them, and re-layouts: 3.37 us -> 3.35 us
where the time goes in v5:
time: 35.2 us; the launch traced here: 35 us
  Pallas kernels  31 us (88%)
  local copies, waits for them, and re-layouts  3.35 us (10%)
  between operations  0.64 us (2%)
    pallas_call x1, Pallas kernels, body(): pl.pallas_call(functools.partial(kernel, n_prompt, n_seq), out_shape=out_...  31 us
    unnamed x4, local copies, waits for them, and re-layouts  3.35 us

profile of v5, /device:TPU:1, one launch (start us, length us, event | category | flops | bytes accessed | tf_op | source)
XLA Modules:
  0.0 35.0 jit_solution(1781192722930347126)
XLA Ops:
  0.6 31.0 %attention_core.1 = (bf16[1,512,1024]{2,1,0:T(8,128)(2,1)S(1)}, bf16[1,512,1024]{2,1,0:T(8,128)(2,1)S(1)}, f32[1,512,256]{2,1,0:T(8,128)S(1)}, f32[1,48,256]{2,1,0:T(8,128)S(1)}) custom-call(s32[1,4]{1,0:T(1,128)} %lens_ref.1, bf16[1,512,1024]{2,1,0:T(8,128)(2,1)} %q_hbm.1, bf16[1,512,256]{2,1,0:T(8,128)(2,1)} %kv_hbm.1, bf16[1,48,256]{2,1,0:T(8,128)(2,1)} %pkv_hbm.1, ...), custom_call_target="tpu_custom_call" | custom-call | tf_op jit(solution)/shard_map/attention_core/pallas_call | solution.py:483
  31.7 1.0 %copy.13 = bf16[1,512,1024]{2,1,0:T(8,128)(2,1)} copy(bf16[1,512,1024]{2,1,0:T(8,128)(2,1)S(1)} %get-tuple-element.8) | data formatting | bytes 2097152
  32.6 1.0 %copy.14 = bf16[1,512,1024]{2,1,0:T(8,128)(2,1)} copy(bf16[1,512,1024]{2,1,0:T(8,128)(2,1)S(1)} %get-tuple-element.9) | data formatting | bytes 2097152
  33.6 0.8 %copy.15 = f32[1,512,256]{2,1,0:T(8,128)} copy(f32[1,512,256]{2,1,0:T(8,128)S(1)} %get-tuple-element.10) | data formatting | bytes 1048576
  34.4 0.6 %copy.16 = f32[1,48,256]{2,1,0:T(8,128)} copy(f32[1,48,256]{2,1,0:T(8,128)S(1)} %get-tuple-element.11) | data formatting | bytes 98304

commit v6 on v5

--- a/solution.py
+++ b/solution.py
@@ -13,7 +13,7 @@
 TILE = 128
 HIDDEN = -1e30
 PAIR = 2
-CHUNK = 128
+CHUNK = 256
 ONES = 16
 
 

time: 35.2 us -> 38.3 us (1.088)
  Pallas kernels: 31 us -> 34.2 us
    pallas_call x1, Pallas kernels: 31 us -> 34.2 us  [body(): pl.pallas_call(functools.partial(kernel, n_prompt, n_seq), out_shape=out_...]
where the time goes in v6:
time: 38.3 us; the launch traced here: 38.2 us
  Pallas kernels  34.2 us (89%)
  local copies, waits for them, and re-layouts  3.35 us (9%)
  between operations  0.64 us (2%)
    pallas_call x1, Pallas kernels, body(): pl.pallas_call(functools.partial(kernel, n_prompt, n_seq), out_shape=out_...  34.2 us
    unnamed x4, local copies, waits for them, and re-layouts  3.35 us

profile of v6, /device:TPU:1, one launch (start us, length us, event | category | flops | bytes accessed | tf_op | source)
XLA Modules:
  0.0 38.2 jit_solution(14149644952269519485)
XLA Ops:
  0.6 34.2 %attention_core.1 = (bf16[1,512,1024]{2,1,0:T(8,128)(2,1)S(1)}, bf16[1,512,1024]{2,1,0:T(8,128)(2,1)S(1)}, f32[1,512,256]{2,1,0:T(8,128)S(1)}, f32[1,48,256]{2,1,0:T(8,128)S(1)}) custom-call(s32[1,4]{1,0:T(1,128)} %lens_ref.1, bf16[1,512,1024]{2,1,0:T(8,128)(2,1)} %q_hbm.1, bf16[1,512,256]{2,1,0:T(8,128)(2,1)} %kv_hbm.1, bf16[1,48,256]{2,1,0:T(8,128)(2,1)} %pkv_hbm.1, ...), custom_call_target="tpu_custom_call" | custom-call | tf_op jit(solution)/shard_map/attention_core/pallas_call | solution.py:483
  34.8 1.0 %copy.13 = bf16[1,512,1024]{2,1,0:T(8,128)(2,1)} copy(bf16[1,512,1024]{2,1,0:T(8,128)(2,1)S(1)} %get-tuple-element.8) | data formatting | bytes 2097152
  35.8 1.0 %copy.14 = bf16[1,512,1024]{2,1,0:T(8,128)(2,1)} copy(bf16[1,512,1024]{2,1,0:T(8,128)(2,1)S(1)} %get-tuple-element.9) | data formatting | bytes 2097152
  36.7 0.8 %copy.15 = f32[1,512,256]{2,1,0:T(8,128)} copy(f32[1,512,256]{2,1,0:T(8,128)S(1)} %get-tuple-element.10) | data formatting | bytes 1048576
  37.5 0.6 %copy.16 = f32[1,48,256]{2,1,0:T(8,128)} copy(f32[1,48,256]{2,1,0:T(8,128)S(1)} %get-tuple-element.11) | data formatting | bytes 98304

commit v7 on v6

--- a/solution.py
+++ b/solution.py
@@ -13,7 +13,7 @@
 TILE = 128
 HIDDEN = -1e30
 PAIR = 2
-CHUNK = 256
+CHUNK = 64
 ONES = 16
 
 
@@ -309,7 +309,7 @@
             ].T
 
     def window(i, lo=0, size=span):
-        return pl.ds(pl.multiple_of(i * TILE + lo, TILE), size)
+        return pl.ds(pl.multiple_of(i * TILE + lo, math.gcd(TILE, lo)), size)
 
     low_rows, top_rows = pl.ds(prefix, span), pl.ds(0, prefix)
     chunks = [(True, lo, min(CHUNK, prefix - lo)) for lo in range(0, prefix, CHUNK)]

time: 38.3 us -> 40.4 us (1.055)
  Pallas kernels: 34.2 us -> 36.3 us
    pallas_call x1, Pallas kernels: 34.2 us -> 36.3 us  [body(): pl.pallas_call(functools.partial(kernel, n_prompt, n_seq), out_shape=out_...]
where the time goes in v7:
time: 40.4 us; the launch traced here: 40.3 us
  Pallas kernels  36.3 us (90%)
  local copies, waits for them, and re-layouts  3.35 us (8%)
  between operations  0.64 us (2%)
    pallas_call x1, Pallas kernels, body(): pl.pallas_call(functools.partial(kernel, n_prompt, n_seq), out_shape=out_...  36.3 us
    unnamed x4, local copies, waits for them, and re-layouts  3.35 us

profile of v7, /device:TPU:1, one launch (start us, length us, event | category | flops | bytes accessed | tf_op | source)
XLA Modules:
  0.0 40.3 jit_solution(12306206541843938098)
XLA Ops:
  0.6 36.3 %attention_core.1 = (bf16[1,512,1024]{2,1,0:T(8,128)(2,1)S(1)}, bf16[1,512,1024]{2,1,0:T(8,128)(2,1)S(1)}, f32[1,512,256]{2,1,0:T(8,128)S(1)}, f32[1,48,256]{2,1,0:T(8,128)S(1)}) custom-call(s32[1,4]{1,0:T(1,128)} %lens_ref.1, bf16[1,512,1024]{2,1,0:T(8,128)(2,1)} %q_hbm.1, bf16[1,512,256]{2,1,0:T(8,128)(2,1)} %kv_hbm.1, bf16[1,48,256]{2,1,0:T(8,128)(2,1)} %pkv_hbm.1, ...), custom_call_target="tpu_custom_call" | custom-call | tf_op jit(solution)/shard_map/attention_core/pallas_call | solution.py:483
  36.9 1.0 %copy.13 = bf16[1,512,1024]{2,1,0:T(8,128)(2,1)} copy(bf16[1,512,1024]{2,1,0:T(8,128)(2,1)S(1)} %get-tuple-element.8) | data formatting | bytes 2097152
  37.9 1.0 %copy.14 = bf16[1,512,1024]{2,1,0:T(8,128)(2,1)} copy(bf16[1,512,1024]{2,1,0:T(8,128)(2,1)S(1)} %get-tuple-element.9) | data formatting | bytes 2097152
  38.9 0.8 %copy.15 = f32[1,512,256]{2,1,0:T(8,128)} copy(f32[1,512,256]{2,1,0:T(8,128)S(1)} %get-tuple-element.10) | data formatting | bytes 1048576
  39.7 0.6 %copy.16 = f32[1,48,256]{2,1,0:T(8,128)} copy(f32[1,48,256]{2,1,0:T(8,128)S(1)} %get-tuple-element.11) | data formatting | bytes 98304

commit v8 on v7

--- a/solution.py
+++ b/solution.py
@@ -13,7 +13,7 @@
 TILE = 128
 HIDDEN = -1e30
 PAIR = 2
-CHUNK = 64
+CHUNK = 128
 ONES = 16
 
 
@@ -312,14 +312,16 @@
         return pl.ds(pl.multiple_of(i * TILE + lo, math.gcd(TILE, lo)), size)
 
     low_rows, top_rows = pl.ds(prefix, span), pl.ds(0, prefix)
-    chunks = [(True, lo, min(CHUNK, prefix - lo)) for lo in range(0, prefix, CHUNK)]
+    first_size = CHUNK + prefix % CHUNK
+    chunks = [(True, 0, first_size)]
+    chunks += [(True, lo, CHUNK) for lo in range(first_size, prefix, CHUNK)]
     chunks += [(False, lo, min(CHUNK, span - lo)) for lo in range(0, span, CHUNK)]
 
     def pipeline_step(u):
         a_tile, a_pair = place(u)
         b_tile, b_pair = place(u - 1)
         c_tile, c_pair = place(u - 2)
-        q_a = jnp.concatenate(heads_of(q_ref, a_pair, a_tile), axis=0)
+        q_a = jnp.concatenate([v.T for v in heads_of(q_ref, a_pair, a_tile)], axis=1)
         q_c = jnp.concatenate(heads_of(q_ref, c_pair, c_tile), axis=0)
         b_top = jnp.max(top_ref[...], axis=0, keepdims=True)
         g_c = g_ref[...]
@@ -339,7 +341,7 @@
             dp = mm(values, g_c) - delta_c
             d_ref[at] = (w_ref[at].astype(F32) * dp).astype(BF16)
             w_ref[at] = jnp.exp2((s_ref[at] - b_top) * step_scale).astype(BF16)
-            score = mm_nt(keys, q_a)
+            score = mm(keys, q_a)
             if not in_prefix:
                 score = score + jnp.concatenate([bias[pl.ds(lo, size)]] * PAIR, axis=1)
             s_ref[at] = score

time: 40.4 us -> 38.5 us (0.953)
  Pallas kernels: 36.3 us -> 34.4 us
    pallas_call x1, Pallas kernels: 36.3 us -> 34.4 us  [body(): pl.pallas_call(functools.partial(kernel, n_prompt, n_seq), out_shape=out_...]
where the time goes in v8:
time: 38.5 us; the launch traced here: 38.4 us
  Pallas kernels  34.4 us (89%)
  local copies, waits for them, and re-layouts  3.35 us (9%)
  between operations  0.64 us (2%)
    pallas_call x1, Pallas kernels, body(): pl.pallas_call(functools.partial(kernel, n_prompt, n_seq), out_shape=out_...  34.4 us
    unnamed x4, local copies, waits for them, and re-layouts  3.35 us

profile of v8, /device:TPU:1, one launch (start us, length us, event | category | flops | bytes accessed | tf_op | source)
XLA Modules:
  0.0 38.4 jit_solution(15687856922567922162)
XLA Ops:
  0.6 34.4 %attention_core.1 = (bf16[1,512,1024]{2,1,0:T(8,128)(2,1)S(1)}, bf16[1,512,1024]{2,1,0:T(8,128)(2,1)S(1)}, f32[1,512,256]{2,1,0:T(8,128)S(1)}, f32[1,48,256]{2,1,0:T(8,128)S(1)}) custom-call(s32[1,4]{1,0:T(1,128)} %lens_ref.1, bf16[1,512,1024]{2,1,0:T(8,128)(2,1)} %q_hbm.1, bf16[1,512,256]{2,1,0:T(8,128)(2,1)} %kv_hbm.1, bf16[1,48,256]{2,1,0:T(8,128)(2,1)} %pkv_hbm.1, ...), custom_call_target="tpu_custom_call" | custom-call | tf_op jit(solution)/shard_map/attention_core/pallas_call | solution.py:485
  35.0 1.0 %copy.13 = bf16[1,512,1024]{2,1,0:T(8,128)(2,1)} copy(bf16[1,512,1024]{2,1,0:T(8,128)(2,1)S(1)} %get-tuple-element.8) | data formatting | bytes 2097152
  36.0 1.0 %copy.14 = bf16[1,512,1024]{2,1,0:T(8,128)(2,1)} copy(bf16[1,512,1024]{2,1,0:T(8,128)(2,1)S(1)} %get-tuple-element.9) | data formatting | bytes 2097152
  36.9 0.8 %copy.15 = f32[1,512,256]{2,1,0:T(8,128)} copy(f32[1,512,256]{2,1,0:T(8,128)S(1)} %get-tuple-element.10) | data formatting | bytes 1048576
  37.7 0.6 %copy.16 = f32[1,48,256]{2,1,0:T(8,128)} copy(f32[1,48,256]{2,1,0:T(8,128)S(1)} %get-tuple-element.11) | data formatting | bytes 98304
